TPU v7x, 32 devices: a whole 2x2x4 slice. The times are simulated.
32 devices in a mesh: groups: 2 (over y), seq: 4 (over z), rows: 2 (over x), cfg: 2 (over core).
Axes of the slice: x: 2, y: 2, z: 4, core: 2. Of those that a mesh axis runs over, the one named last changes fastest.
Arguments:
- hidden: bfloat16 [2, 4096, 5120], P('cfg', ('groups', 'seq', 'rows')), parts along dimension 1, may hold values from -500 to 500
- token_order: int32 [4096], P(('groups', 'seq', 'rows')), parts along dimension 0, may hold values from 0 to 2047, as said below
- noisy_latent: float32 [16, 8, 2048], P(('groups', 'seq'), ('rows', 'cfg')), parts along dimension 0, may hold values from -6 to 6
- head_weight: bfloat16 [5120, 64], replicated, may hold values from -0.078125 to 0.078125
- head_mod: float32 [2, 5120], replicated, may hold values from -2.5 to 2.5
- guidance: float32 [1], replicated, may hold values from 3 to 7
- timestep_index: int32 [1], replicated, may hold values from 0 to 7
- step_table: int32 [9], replicated, may hold values from 0 to 1000, as said below
- vae_mean: float32 [16], replicated, may hold values from -2.5 to 2.5
- vae_std: float32 [16], replicated, may hold values from 1.1 to 3.3
- conv2_weight: float32 [16, 16], replicated, may hold values from -1.5 to 1.5
- conv2_bias: float32 [16], replicated, may hold values from -2.5 to 2.5
- conv1_weight: bfloat16 [27, 16, 384], replicated, may hold values from -0.3125 to 0.3125
- conv1_bias: float32 [384], replicated, may hold values from -2.5 to 2.5
Outputs:
- decoded: bfloat16 [16, 8, 128, 384], P(('groups', 'seq'), ('rows', 'cfg')), parts along dimension 0
There are 2 independent parts, one for each index of `groups`. A program takes and returns all parts, laid end to end along the dimension named above; an argument that names none is the same for every part. Nothing has to cross between parts.
Inputs may be any that keep to these rules, and one draw needn't show every extreme that they name: `token_order`: a permutation of the 2048 cells, cell f * 4 * 64 + i * 64 + j being token column j of token row i of frame f; positions k * 256 to (k + 1) * 256 - 1 with k = s * 2 + r hold exactly the cells of frames s * 2 to (s + 1) * 2 - 1 and token rows r * 2 to (r + 1) * 2 - 1. `step_table`: strictly decreasing from 1000 to 0; consecutive entries differ by 90 or more.
All inputs are finite; a program needn't handle non-finite values.
Results may differ from a plain program's by a relative error of at most 0.0053.
Values may be sent and summed in bfloat16 or wider, within the bound.
A program may use at most 64 MiB of HBM per device.

v0:
```python
import jax
import jax.numpy as jnp
from jax import lax
from jax.sharding import PartitionSpec as P

FR_DEV = 2
TR_DEV = 2
WT = 64


def padded_2(block, sides, width):
    for axis, dim in sides:
        count = lax.axis_size(axis)
        forward = [(i, i + 1) for i in range(count - 1)]
        backward = [(target, source) for source, target in forward]
        low = lax.ppermute(
            lax.slice_in_dim(block, block.shape[dim] - width, None, axis=dim), axis, forward
        )
        high = lax.ppermute(lax.slice_in_dim(block, 0, width, axis=dim), axis, backward)
        block = jnp.concatenate([low, block, high], axis=dim)
    return block


def shifted(block, axis, distance):
    devices = range(lax.axis_size(axis))
    route = [(i - distance, i) for i in devices if i - distance in devices]
    return lax.ppermute(block, axis, route)


def head_rows(row_block, head_weight, head_mod):
    values = row_block.astype(jnp.float32)
    center = jnp.mean(values, axis=-1, keepdims=True)
    spread = jnp.mean(jnp.square(values - center), axis=-1, keepdims=True)
    normed = (values - center) * lax.rsqrt(spread + 1e-06)
    head_in = (normed * (1.0 + head_mod[1]) + head_mod[0]).astype(jnp.bfloat16)
    return jnp.dot(head_in, head_weight, preferred_element_type=jnp.float32)


def conv_taps(padded, frames, row_count, col_count):
    pieces = []
    for step_time in range(3):
        for step_row in range(3):
            for step_col in range(3):
                pieces.append(
                    padded[
                        step_time : step_time + frames,
                        step_row : step_row + row_count,
                        step_col : step_col + col_count,
                        :,
                    ]
                )
    return jnp.concatenate(pieces, axis=-1)


def per_device(
    hidden,
    token_order,
    noisy_latent,
    head_weight,
    head_mod,
    guidance,
    timestep_index,
    step_table,
    vae_mean,
    vae_std,
    conv2_weight,
    conv2_bias,
    conv1_weight,
    conv1_bias,
):
    token_count = hidden.shape[1]
    patch_width = head_weight.shape[1]
    lat_channels = vae_mean.shape[0]
    out_channels = conv1_weight.shape[2]
    token_rows = TR_DEV * lax.axis_size("rows")
    own_head = head_rows(hidden[0], head_weight, head_mod)
    frame_pos = token_order // (token_rows * WT) % FR_DEV
    row_pos = token_order // WT % TR_DEV
    col_pos = token_order % WT
    local_cell = (frame_pos * TR_DEV + row_pos) * WT + col_pos
    placed = jnp.zeros((token_count, patch_width), jnp.float32).at[local_cell].set(own_head)
    local_block = placed.reshape(FR_DEV, TR_DEV, WT, 2, 2, lat_channels).transpose(0, 1, 3, 2, 4, 5)
    local_block = local_block.reshape(FR_DEV, 2, TR_DEV, 2 * WT * lat_channels)
    gathered = lax.all_gather(local_block[None], "cfg", axis=0, tiled=True)
    half_index = lax.axis_index("cfg")
    conditional = lax.dynamic_index_in_dim(gathered[0], half_index, 1, keepdims=False)
    unconditional = lax.dynamic_index_in_dim(gathered[1], half_index, 1, keepdims=False)
    velocity = unconditional + guidance[0] * (conditional - unconditional)
    step_index = timestep_index[0]
    sigma_now = step_table[step_index].astype(jnp.float32) / 1000.0
    sigma_next = step_table[step_index + 1].astype(jnp.float32) / 1000.0
    stepped = noisy_latent + (sigma_next - sigma_now) * velocity
    channels = stepped.reshape(FR_DEV, TR_DEV, 2 * WT, lat_channels) * vae_std + vae_mean
    mixed_lat = (
        jnp.einsum("fyxc,cd->fyxd", channels, conv2_weight, precision=lax.Precision.HIGHEST)
        + conv2_bias
    )
    latent_in = mixed_lat.astype(jnp.bfloat16).reshape(FR_DEV, TR_DEV, 2 * WT * lat_channels)
    framed = padded_2(latent_in, ((("rows", "cfg"), 1),), 1)
    earlier = shifted(framed, "seq", 1)
    padded = jnp.concatenate([earlier, framed], axis=0).reshape(
        FR_DEV + 2, TR_DEV + 2, 2 * WT, lat_channels
    )
    padded = jnp.pad(padded, ((0, 0), (0, 0), (1, 1), (0, 0)))
    tap_columns = conv_taps(padded, FR_DEV, TR_DEV, 2 * WT).reshape(
        FR_DEV * TR_DEV * 2 * WT, 27 * lat_channels
    )
    kernel = conv1_weight.reshape(27 * lat_channels, out_channels)
    result = jnp.dot(tap_columns, kernel, preferred_element_type=jnp.float32) + conv1_bias
    return result.astype(jnp.bfloat16).reshape(FR_DEV, TR_DEV, 2 * WT, out_channels)


def solution(mesh):
    return jax.shard_map(
        per_device,
        mesh=mesh,
        in_specs=(
            P("cfg", ("groups", "seq", "rows"), None),
            P(("groups", "seq", "rows")),
            P(("groups", "seq"), ("rows", "cfg"), None),
            P(),
            P(),
            P(),
            P(),
            P(),
            P(),
            P(),
            P(),
            P(),
            P(),
            P(),
        ),
        out_specs=P(("groups", "seq"), ("rows", "cfg"), None, None),
        check_vma=False,
    )
```

profile of v0, /device:TPU:1, one launch (start us, length us, event | category | flops | bytes accessed | tf_op | source)
XLA Modules:
  0.0 36.1 jit_solution(17837188760740041675)
XLA Ops:
  0.8 1.4 %fusion.30 = (s32[1]{0:T(128)}, s32[1]{0:T(128)}) fusion(s32[9]{0:T(128)} %param.21, s32[]{:T(128)S(6)} %select_n.38, s32[]{:T(128)S(6)} %select_n.37), kind=kLoop, calls=%fused_computation.73 | loop fusion | bytes 24 | tf_op jit(solution)/shard_map/dynamic_slice | solution.py:90
  3.5 0.9 %slice_add_fusion = (f32[1,5120]{1,0:T(1,128)S(1)}, f32[1,5120]{1,0:T(1,128)S(1)}) fusion(f32[2,5120]{1,0:T(2,128)} %param.18), kind=kLoop, calls=%fused_computation.26 | loop fusion | flops 5120 | bytes 81920 | tf_op jit(solution)/shard_map/add | solution.py:35
  4.4 2.2 %convert_reduce_fusion = f32[256]{0:T(256)S(1)} fusion(bf16[1,256,5120]{2,1,0:T(8,128)(2,1)} %param.14), kind=kLoop, calls=%fused_computation.1 | loop fusion | flops 2621184 | bytes 2622464 | tf_op jit(solution)/shard_map/reduce_sum | solution.py:32
  6.6 0.8 %fusion.3 = f32[256]{0:T(256)S(1)} fusion(bf16[1,256,5120]{2,1,0:T(8,128)(2,1)S(1)} %copy-done.1, f32[256]{0:T(256)S(1)} %broadcast_multiply_fusion), kind=kLoop, calls=%fused_computation.6 | loop fusion | flops 5242624 | bytes 2623488 | tf_op jit(solution)/shard_map/reduce_sum | solution.py:33
  7.5 1.1 %fusion.7 = f32[256,64]{1,0:T(8,128)S(1)} fusion(bf16[5120,64]{0,1:T(8,128)(2,1)S(1)} %copy-done, bf16[1,256,5120]{2,1,0:T(8,128)(2,1)S(1)} %copy-done.1, f32[5120]{0:T(1024)S(1)} %bitcast.57, f32[5120]{0:T(1024)S(1)} %bitcast.56, f32[256]{0:T(256)S(1)} %add_rsqrt_fusion, f32[256]{0:T(256)S(1)} %broadcast_multiply_fusion), kind=kOutput, calls=%fused_computation.10 | convolution fusion | flops 175636480 | bytes 3385344 | tf_op jit(solution)/shard_map/dot_general | solution.py:36
  8.7 1.2 %scatter_custom_fusion = f32[256,64]{1,0:T(8,128)S(1)} fusion(s32[256]{0:T(256)S(1)} %compare_select_fusion, f32[256,64]{1,0:T(8,128)S(1)} %fusion.7, f32[]{:T(128)} %constant.82.clone.1), kind=kCustom, calls=%fused_computation.16 | custom fusion | bytes 65540 | tf_op jit(solution)/shard_map/scatter | solution.py:81
  10.1 0.3 copy.31
  10.4 0.7 %broadcast_in_dim_reshape.3 = f32[1,2,2,2,2048]{4,3,2,1,0:T(2,128)S(1)} reshape(f32[2,2,2,64,2,16]{5,4,3,2,1,0:T(2,128)S(1)} %copy.31) | data formatting | bytes 131072 | tf_op jit(solution)/shard_map/broadcast_in_dim;reshape | solution.py:84
  11.1 1.9 %all_gather.3 = f32[2,2,2,2,2048]{4,3,2,1,0:T(2,128)S(1)} all-gather(f32[1,2,2,2,2048]{4,3,2,1,0:T(2,128)S(1)} %broadcast_in_dim_reshape.3), channel_id=1, replica_groups=mesh['groups'=2,'seq'=4,'rows'=2,'cfg'=2] {'cfg'}, dimensions={0}, use_global_device_ids=true | all-gather | bytes 196608 | tf_op jit(solution)/shard_map/all_gather | solution.py:84
  13.7 0.1 reshape.50
  14.0 0.2 fusion.10
  14.2 0.1 copy.34
  14.3 0.2 reshape.51
  14.5 4.5 %collective-permute-start = (bf16[2,1,2048]{2,1,0:T(2,128)(2,1)S(1)}, bf16[2,1,2048]{2,1,0:T(2,128)(2,1)S(1)}, u32[]{:S(2)}, u32[]{:S(2)}) collective-permute-start(bf16[2,1,2048]{2,1,0:T(2,128)(2,1)S(1)} %get-tuple-element.36), channel_id=1, source_target_pairs={{0,1},{1,2},{2,3},{4,5},{5,6},{6,7},{8,9},{9,10},{10,11},{12,13},{... | collective-permute-start | bytes 24584 | tf_op jit(solution)/shard_map/ppermute | solution.py:16
  19.1 1.9 %collective-permute-start.1 = (bf16[2,1,2048]{2,1,0:T(2,128)(2,1)S(1)}, bf16[2,1,2048]{2,1,0:T(2,128)(2,1)S(1)}, u32[]{:S(2)}, u32[]{:S(2)}) collective-permute-start(bf16[2,1,2048]{2,1,0:T(2,128)(2,1)S(1)} %get-tuple-element.37), channel_id=1, source_target_pairs={{1,0},{2,1},{3,2},{5,4},{6,5},{7,6},{9,8},{10,9},{11,10},{13,12},{... | collective-permute-start | bytes 24584 | tf_op jit(solution)/shard_map/ppermute | solution.py:19
  21.0 3.1 %collective-permute-done.1 = bf16[2,1,2048]{2,1,0:T(2,128)(2,1)S(1)} collective-permute-done((bf16[2,1,2048]{2,1,0:T(2,128)(2,1)S(1)}, bf16[2,1,2048]{2,1,0:T(2,128)(2,1)S(1)}, u32[]{:S(2)}, u32[]{:S(2)}) %collective-permute-start.1) | collective-permute-done | bytes 8224 | tf_op jit(solution)/shard_map/ppermute | solution.py:19
  24.2 3.2 %collective-permute-start.2 = (bf16[2,4,2048]{2,1,0:T(4,128)(2,1)S(1)}, bf16[2,4,2048]{2,1,0:T(4,128)(2,1)S(1)}, u32[]{:S(2)}, u32[]{:S(2)}) collective-permute-start(bf16[2,4,2048]{2,1,0:T(4,128)(2,1)S(1)} %pad_maximum_fusion), channel_id=1, source_target_pairs={{0,4},{4,8},{8,12},{1,5},{5,9},{9,13},{2,6},{6,10},{10,14},{3,7},{... | collective-permute-start | bytes 98312 | tf_op jit(solution)/shard_map/ppermute | solution.py:27
  27.4 1.0 %collective-permute-done.2 = bf16[2,4,2048]{2,1,0:T(4,128)(2,1)S(1)} collective-permute-done((bf16[2,4,2048]{2,1,0:T(4,128)(2,1)S(1)}, bf16[2,4,2048]{2,1,0:T(4,128)(2,1)S(1)}, u32[]{:S(2)}, u32[]{:S(2)}) %collective-permute-start.2) | collective-permute-done | bytes 32800 | tf_op jit(solution)/shard_map/ppermute | solution.py:27
  28.5 0.4 %reshape.52 = bf16[4,4,128,16]{3,2,1,0:T(8,128)(2,1)S(1)} reshape(bf16[4,4,2048]{2,1,0:T(4,128)(2,1)S(1)} %maximum_maximum_fusion) | data formatting | bytes 131072 | tf_op jit(solution)/shard_map/reshape | solution.py:101
  28.8 0.3 pad_slice_fusion.1
  29.2 1.0 %pad_slice_fusion = (bf16[2,2,128,16]{3,2,1,0:T(8,128)(2,1)S(1)}, bf16[2,2,128,16]{3,2,1,0:T(8,128)(2,1)S(1)}, bf16[2,2,128,16]{3,2,1,0:T(8,128)(2,1)S(1)}, bf16...) fusion(bf16[4,4,128,16]{3,2,1,0:T(8,128)(2,1)S(1)} %reshape.52), kind=kLoop, calls=%fused_computation.52 | loop fusion | bytes 819200 | tf_op jit(solution)/shard_map/slice | solution.py:45
  30.1 0.9 %fusion.27 = (bf16[2,2,128,16]{3,2,1,0:T(8,128)(2,1)}, bf16[2,2,128,16]{3,2,1,0:T(8,128)(2,1)}, bf16[2,2,128,16]{3,2,1,0:T(8,128)(2,1)}, bf16[2,2,128,16]{3,2,1,...) fusion(bf16[4,4,128,16]{3,2,1,0:T(8,128)(2,1)S(1)} %reshape.52), kind=kLoop, calls=%fused_computation.70 | loop fusion | bytes 1277952 | tf_op jit(solution)/shard_map/slice | solution.py:45
  31.0 2.9 %concatenate.11 = bf16[2,2,128,432]{3,2,1,0:T(8,128)(2,1)S(1)} concatenate(bf16[2,2,128,16]{3,2,1,0:T(8,128)(2,1)} %get-tuple-element.31, bf16[2,2,128,16]{3,2,1,0:T(8,128)(2,1)} %get-tuple-element.30, bf16[2,2,128,16]{3,2,1,0:T(8,128)(2,1)S(1)} %get-tuple-element.6, bf16[2,2,128,16]{3,2,1,0:T(8,128)(2,1)S(1)} %get-tuple-element.7, bf16[2,2,128,16]{3,2,1,0:T(8,128)(2,1)} %get-tuple-element.29, ...), dimensions={3} | concatenate | bytes 884736 | tf_op jit(solution)/shard_map/concatenate | solution.py:52
  33.9 2.2 %fusion.9 = bf16[512,384]{1,0:T(8,128)(2,1)} fusion(bf16[512,432]{1,0:T(8,128)(2,1)S(1)} %bitcast.55, bf16[432,384]{1,0:T(8,128)(2,1)} %bitcast.58, f32[384]{0:T(512)S(1)} %copy-done.5), kind=kOutput, calls=%fused_computation.12 | convolution fusion | flops 170262528 | bytes 1168896 | tf_op jit(solution)/shard_map/dot_general | solution.py:109
  (30 shorter events, 0.6 us)
Async XLA Ops:
  0.0 7.5 %copy-start = (bf16[5120,64]{0,1:T(8,128)(2,1)S(1)}, bf16[5120,64]{0,1:T(8,128)(2,1)}, u32[]{:S(2)}) copy-start(bf16[5120,64]{0,1:T(8,128)(2,1)} %param.17) | copy-start | bytes 1966084
  0.0 6.6 %copy-start.1 = (bf16[1,256,5120]{2,1,0:T(8,128)(2,1)S(1)}, bf16[1,256,5120]{2,1,0:T(8,128)(2,1)}, u32[]{:S(2)}) copy-start(bf16[1,256,5120]{2,1,0:T(8,128)(2,1)} %param.14) | copy-start | bytes 7864324
  4.4 3.0 %copy-start.3 = (s32[256]{0:T(256)S(1)}, s32[256]{0:T(256)}, u32[]{:S(2)}) copy-start(s32[256]{0:T(256)} %param.15) | copy-start | bytes 3076
  7.5 6.2 %copy-start.2 = (f32[2,2,2048]{2,1,0:T(2,128)S(1)}, f32[2,2,2048]{2,1,0:T(2,128)}, u32[]{:S(2)}) copy-start(f32[2,2,2048]{2,1,0:T(2,128)} %param.16) | copy-start | bytes 98308
  8.6 5.3 %copy-start.4 = (f32[16,16]{1,0:T(8,128)S(1)}, f32[16,16]{1,0:T(8,128)}, u32[]{:S(2)}) copy-start(f32[16,16]{1,0:T(8,128)} %param.24) | copy-start | bytes 3076
  8.7 5.3 %copy-start.6 = (f32[16]{0:T(128)S(1)}, f32[16]{0:T(128)}, u32[]{:S(2)}) copy-start(f32[16]{0:T(128)} %param.25) | copy-start | bytes 196
  8.7 5.3 %copy-start.7 = (f32[16]{0:T(128)S(1)}, f32[16]{0:T(128)}, u32[]{:S(2)}) copy-start(f32[16]{0:T(128)} %param.22) | copy-start | bytes 196
  8.7 5.3 %copy-start.8 = (f32[16]{0:T(128)S(1)}, f32[16]{0:T(128)}, u32[]{:S(2)}) copy-start(f32[16]{0:T(128)} %param.23) | copy-start | bytes 196
  14.5 6.4 %collective-permute-start = (bf16[2,1,2048]{2,1,0:T(2,128)(2,1)S(1)}, bf16[2,1,2048]{2,1,0:T(2,128)(2,1)S(1)}, u32[]{:S(2)}, u32[]{:S(2)}) collective-permute-start(bf16[2,1,2048]{2,1,0:T(2,128)(2,1)S(1)} %get-tuple-element.36), channel_id=1, source_target_pairs={{0,1},{1,2},{2,3},{4,5},{5,6},{6,7},{8,9},{9,10},{10,11},{12,13},{... | collective-permute-start | bytes 24584 | tf_op jit(solution)/shard_map/ppermute | solution.py:16
  19.1 5.1 %collective-permute-start.1 = (bf16[2,1,2048]{2,1,0:T(2,128)(2,1)S(1)}, bf16[2,1,2048]{2,1,0:T(2,128)(2,1)S(1)}, u32[]{:S(2)}, u32[]{:S(2)}) collective-permute-start(bf16[2,1,2048]{2,1,0:T(2,128)(2,1)S(1)} %get-tuple-element.37), channel_id=1, source_target_pairs={{1,0},{2,1},{3,2},{5,4},{6,5},{7,6},{9,8},{10,9},{11,10},{13,12},{... | collective-permute-start | bytes 24584 | tf_op jit(solution)/shard_map/ppermute | solution.py:19
  24.2 4.2 %collective-permute-start.2 = (bf16[2,4,2048]{2,1,0:T(4,128)(2,1)S(1)}, bf16[2,4,2048]{2,1,0:T(4,128)(2,1)S(1)}, u32[]{:S(2)}, u32[]{:S(2)}) collective-permute-start(bf16[2,4,2048]{2,1,0:T(4,128)(2,1)S(1)} %pad_maximum_fusion), channel_id=1, source_target_pairs={{0,4},{4,8},{8,12},{1,5},{5,9},{9,13},{2,6},{6,10},{10,14},{3,7},{... | collective-permute-start | bytes 98312 | tf_op jit(solution)/shard_map/ppermute | solution.py:27
  30.1 3.8 %copy-start.5 = (f32[384]{0:T(512)S(1)}, f32[384]{0:T(512)}, u32[]{:S(2)}) copy-start(f32[384]{0:T(512)} %param.27) | copy-start | bytes 4612
where the time goes:
time: 36.6 us; the launch traced here: 36.1 us
  local copies, waits for them, and re-layouts  9.76 us (27%)
  starting transfers between devices  9.63 us (26%)
  waiting for transfers between devices  4.13 us (11%)
  other arithmetic  4.12 us (11%)
  matrix products  3.55 us (10%)
  between operations  2.99 us (8%)
  blocking collectives  1.9 us (5%)
    ppermute x1, starting transfers between devices, padded_2(): lax.ppermute(lax.slice_in_dim(block, block.shape[dim] - width, None, axis...  4.51 us
    ppermute x1, starting transfers between devices, shifted(): return lax.ppermute(block, axis, route)  3.2 us
    ppermute x1, waiting for transfers between devices, padded_2(): lax.ppermute(lax.slice_in_dim(block, 0, width, axis=dim), axis, backward)  3.12 us
    concatenate x1, local copies, waits for them, and re-layouts, conv_taps(): return jnp.concatenate(pieces, axis=-1)  2.88 us
    reduce_sum x1, other arithmetic, head_rows(): center = jnp.mean(values, axis=-1, keepdims=True)  2.18 us
    slice x3, local copies, waits for them, and re-layouts, conv_taps(): padded[step_time:step_time + frames, step_row:step_row + row_count, step_...  2.17 us
    dot_general x1, matrix products, per_device(): jnp.dot(tap_columns, kernel, preferred_element_type=jnp.float32)  2.16 us
    ppermute x1, starting transfers between devices, padded_2(): lax.ppermute(lax.slice_in_dim(block, 0, width, axis=dim), axis, backward)  1.92 us
  transfers between devices with their start and end apart: 3, of which 2 were waited for; matrix products, arithmetic and copies ran while one was open for 0% of the time, Pallas kernels for 0%

commit v1 on v0

v1 whole, which is shorter than its diff:
```python
import functools

import jax
import jax.numpy as jnp
from jax import lax
from jax.experimental import pallas as pl
from jax.experimental.pallas import tpu as pltpu
from jax.sharding import PartitionSpec as P

F32 = jnp.float32
BF16 = jnp.bfloat16
LANES = 128
EXTRA = 16


def split_bf16(value):
    high = value.astype(BF16)
    low = (value - high.astype(F32)).astype(BF16)
    return high, low


def dot_nt(left, right):
    return lax.dot_general(left, right, (((1,), (1,)), ((), ())), preferred_element_type=F32)


def dot_nn(left, right):
    return jnp.dot(left, right, preferred_element_type=F32)


def kernel(
    sizes,
    hidden_hbm,
    order_hbm,
    noisy_hbm,
    weight_hbm,
    mod_hbm,
    guidance_hbm,
    index_hbm,
    table_hbm,
    mean_hbm,
    std_hbm,
    mix_hbm,
    mix_bias_hbm,
    conv_hbm,
    conv_bias_hbm,
    out_ref,
    x_buf,
    w_buf,
    rhs_buf,
    order_buf,
    noisy_buf,
    mod_buf,
    guidance_buf,
    index_buf,
    table_buf,
    mean_buf,
    std_buf,
    mix_buf,
    mix_bias_buf,
    conv_buf,
    conv_bias_buf,
    latent_buf,
    taps_buf,
    cells_buf,
    partner_buf,
    edge_buf,
    halo_buf,
    wide_buf,
    local_sem,
    chunk_sem,
    send_sem,
    recv_sem,
):
    seq_count, row_count, cfg_count, token_rows, token_cols, frames, chunks = sizes
    tokens = hidden_hbm.shape[1]
    width = hidden_hbm.shape[2]
    patch = weight_hbm.shape[0]
    chan = mix_hbm.shape[0]
    out_chan = conv_hbm.shape[2]
    slab_count = row_count * cfg_count
    step = width // chunks

    seq = lax.axis_index("seq")
    row = lax.axis_index("rows")
    half = lax.axis_index("cfg")
    slab = row * cfg_count + half

    small = []
    for source, target in (
        (mod_hbm, mod_buf),
        (order_hbm, order_buf),
        (noisy_hbm, noisy_buf),
        (guidance_hbm, guidance_buf),
        (index_hbm, index_buf),
        (table_hbm, table_buf),
        (mean_hbm, mean_buf),
        (std_hbm, std_buf),
        (mix_hbm, mix_buf),
        (mix_bias_hbm, mix_bias_buf),
        (conv_bias_hbm, conv_bias_buf),
        (conv_hbm, conv_buf),
    ):
        small.append(pltpu.make_async_copy(source, target, local_sem.at[len(small)]))
    loads = []
    for part in range(chunks):
        columns = pl.ds(part * step, step)
        loads.append(
            (
                pltpu.make_async_copy(
                    weight_hbm.at[:, columns], w_buf.at[:, columns], chunk_sem.at[0, part]
                ),
                pltpu.make_async_copy(
                    hidden_hbm.at[0, :, columns],
                    x_buf.at[pl.ds(0, tokens), columns],
                    chunk_sem.at[1, part],
                ),
            )
        )
    small[0].start()
    for weight_copy, hidden_copy in loads:
        weight_copy.start()
        hidden_copy.start()
    for copy in small[1:]:
        copy.start()

    barrier = pltpu.get_barrier_semaphore()

    def present(seq_step, slab_step):
        ok = jnp.bool_(True)
        if seq_step:
            ok = jnp.logical_and(ok, seq > 0 if seq_step < 0 else seq < seq_count - 1)
        if slab_step:
            ok = jnp.logical_and(ok, slab > 0 if slab_step < 0 else slab < slab_count - 1)
        return ok

    def place(seq_step, slab_step):
        other = slab + slab_step + cfg_count
        return {
            "seq": seq + seq_step,
            "rows": lax.div(other, cfg_count) - 1,
            "cfg": lax.rem(other, cfg_count),
        }

    around = [(a, b) for a in (-1, 0, 1) for b in (-1, 0, 1) if a or b]
    for offset in around:

        @pl.when(present(*offset))
        def _(offset=offset):
            pl.semaphore_signal(
                barrier, inc=1, device_id=place(*offset), device_id_type=pl.DeviceIdType.MESH
            )

    sends = ((0, 1), (0, -1), (1, 0), (1, 1), (1, -1))
    for slot, (seq_step, slab_step) in enumerate(sends):

        @pl.when(jnp.logical_not(present(-seq_step, -slab_step)))
        def _(slot=slot):
            halo_buf[slot] = jnp.zeros(halo_buf.shape[1:], BF16)

    small[0].wait()
    scale = 1.0 + mod_buf[1:2, :]
    shift_high, shift_low = split_bf16(mod_buf[0:1, :])
    pick = lax.broadcasted_iota(jnp.int32, (EXTRA, width), 0)
    x_buf[tokens : tokens + EXTRA, :] = jnp.where(
        pick == 0,
        shift_high.astype(F32),
        jnp.where(pick == 1, shift_low.astype(F32), jnp.where(pick == 2, 1.0, 0.0)),
    ).astype(BF16)
    ones_row = lax.broadcasted_iota(jnp.int32, (EXTRA, width), 0) == 0
    rhs_buf[2 * patch : 2 * patch + EXTRA, :] = jnp.where(ones_row, 1.0, 0.0).astype(BF16)

    block = 64
    blocks = tokens // block
    product = jnp.zeros((tokens + EXTRA, rhs_buf.shape[0]), F32)
    centers = [None] * blocks
    squares = [jnp.zeros((block, LANES), F32)] * blocks
    for part, (weight_copy, hidden_copy) in enumerate(loads):
        low = part * step
        weight_copy.wait()
        raw = w_buf[:, low : low + step]
        rhs_buf[0:patch, low : low + step] = (
            raw.astype(F32) * scale[:, low : low + step]
        ).astype(BF16)
        rhs_buf[patch : 2 * patch, low : low + step] = raw
        hidden_copy.wait()
        product = product + dot_nt(x_buf[:, low : low + step], rhs_buf[:, low : low + step])
        for index in range(blocks):
            rows = slice(index * block, (index + 1) * block)
            if part == 0:
                total = jnp.zeros((block, LANES), F32)
                for lane in range(0, step, LANES):
                    total = total + x_buf[rows, lane : lane + LANES].astype(F32)
                center = jnp.sum(total, axis=1, keepdims=True) * (1.0 / step)
                centers[index] = jnp.broadcast_to(center, (block, LANES))
            square = squares[index]
            for lane in range(low, low + step, LANES):
                gap = x_buf[rows, lane : lane + LANES].astype(F32) - centers[index]
                square = square + gap * gap
            squares[index] = square

    center = jnp.concatenate([value[:, 0:1] for value in centers], axis=0)
    spread = jnp.concatenate([jnp.sum(value, axis=1, keepdims=True) for value in squares], axis=0)
    average = product[0:tokens, 2 * patch : 2 * patch + 1] * (1.0 / width)
    spread = spread * (1.0 / width) - jnp.square(average - center)
    inverse = lax.rsqrt(spread + 1e-06)
    column_sum = product[tokens + 2 : tokens + 3, 0:patch]
    both = product[tokens : tokens + 1, :] + product[tokens + 1 : tokens + 2, :]
    offset_row = both[:, patch : 2 * patch]
    head = (product[0:tokens, 0:patch] - average * column_sum) * inverse + offset_row

    for copy in small[1:]:
        copy.wait()
    cell = order_buf[...].astype(F32) + 0.5
    per_frame = float(row_count * token_rows * token_cols)
    frame_all = jnp.floor(cell * (1.0 / per_frame))
    in_frame = cell - frame_all * per_frame
    frame_pos = frame_all - frames * jnp.floor((frame_all + 0.5) * (1.0 / frames))
    row_all = jnp.floor(in_frame * (1.0 / token_cols))
    column = in_frame - 0.5 - row_all * token_cols
    row_pos = row_all - token_rows * jnp.floor((row_all + 0.5) * (1.0 / token_rows))
    target = (frame_pos * token_rows + row_pos) * token_cols + column
    wanted = lax.broadcasted_iota(jnp.int32, (tokens, tokens), 0).astype(F32)
    one_hot = jnp.where(jnp.abs(wanted - target) < 0.25, 1.0, 0.0).astype(BF16)
    head_high, head_low = split_bf16(head)
    placed = dot_nn(one_hot, head_high) + dot_nn(one_hot, head_low)
    per = token_rows * token_cols
    for index in range(token_rows):
        pieces = [
            placed[f * per + index * token_cols : f * per + (index + 1) * token_cols, :]
            for f in range(frames)
        ]
        cells_buf[index] = jnp.concatenate(pieces, axis=1)

    slab_peers = (slab > 0).astype(jnp.int32) + (slab < slab_count - 1).astype(jnp.int32)
    seq_peers = (seq > 0).astype(jnp.int32) + (seq < seq_count - 1).astype(jnp.int32)
    pl.semaphore_wait(barrier, (1 + slab_peers) * (1 + seq_peers) - 1)

    pair = pltpu.make_async_remote_copy(
        src_ref=cells_buf.at[1 - half],
        dst_ref=partner_buf,
        send_sem=send_sem.at[0],
        recv_sem=recv_sem.at[0],
        device_id={"cfg": 1 - half},
        device_id_type=pl.DeviceIdType.MESH,
    )
    pair.start()

    lane = lax.broadcasted_iota(jnp.int32, (noisy_buf.shape[2], LANES), 1)
    span = 2 * chan
    per_line = LANES // span
    groups = noisy_buf.shape[2]
    for jj in range(per_line):
        line = jnp.zeros((groups, LANES), F32)
        for f in range(frames):
            for a in range(2):
                slot = f * 2 + a
                moved = noisy_buf[f, a]
                if (slot - jj) % per_line:
                    moved = pltpu.roll(moved, ((slot - jj) * span) % LANES, 1)
                line = jnp.where((lane >= slot * span) & (lane < (slot + 1) * span), moved, line)
        latent_buf[pl.ds(jj, groups, stride=per_line), :] = line

    repeat = LANES // chan

    def lanes_of(ref):
        return jnp.concatenate([ref[...]] * repeat, axis=1)

    mean_row = lanes_of(mean_buf)
    std_row = lanes_of(std_buf)
    mix_row = lanes_of(mix_bias_buf)
    mix = jnp.concatenate([lanes_of(mix_buf)] * repeat, axis=0)
    mix_in = lax.broadcasted_iota(jnp.int32, (LANES, LANES), 0)
    mix_out = lax.broadcasted_iota(jnp.int32, (LANES, LANES), 1)
    same = lax.div(mix_in, chan) == lax.div(mix_out, chan)
    mix_high, mix_low = split_bf16(jnp.where(same, mix, 0.0))
    mix_both = jnp.concatenate([mix_high, mix_low], axis=1)

    spot = lax.broadcasted_iota(jnp.int32, table_buf.shape, 1)
    table = table_buf[...].astype(F32)
    now = jnp.sum(jnp.where(spot == index_buf[...], table, 0.0), axis=1, keepdims=True)
    later = jnp.sum(jnp.where(spot == index_buf[...] + 1, table, 0.0), axis=1, keepdims=True)
    step_size = later / 1000.0 - now / 1000.0

    position = 0
    for t in range(3):
        for shifted in range(2):
            for u in range(4):
                for e_in in range(2):
                    dx = (2 - 3 * e_in) if shifted else e_in
                    for e_out in range(2):
                        w = dx - e_out + 1
                        columns = slice(e_out * out_chan, (e_out + 1) * out_chan)
                        if u < 3 and 0 <= w <= 2:
                            value = conv_buf[(t * 3 + u) * 3 + w]
                        else:
                            value = jnp.zeros((chan, out_chan), BF16)
                        taps_buf[position : position + chan, columns] = value
                    position += chan

    pair.wait_recv()
    own = cells_buf[half]
    partner = partner_buf[...]
    cond = jnp.where(half == 0, own, partner)
    free = jnp.where(half == 0, partner, own)
    velocity = free + guidance_buf[...] * (cond - free)
    stepped = latent_buf[...] + step_size * velocity
    channels = stepped * std_row + mean_row
    high, low = split_bf16(channels)
    mixed = dot_nn(jnp.concatenate([high, low], axis=0), mix_both)
    mixed = mixed[0:token_cols, 0:LANES] + (
        mixed[0:token_cols, LANES:] + mixed[token_cols:, 0:LANES]
    )
    latent = (mixed + mix_row).astype(BF16)
    edge_buf[...] = latent

    copies = []
    for slot, (seq_step, slab_step) in enumerate(sends):
        copy = pltpu.make_async_remote_copy(
            src_ref=edge_buf,
            dst_ref=halo_buf.at[slot],
            send_sem=send_sem.at[1 + slot],
            recv_sem=recv_sem.at[1 + slot],
            device_id=place(seq_step, slab_step),
            device_id_type=pl.DeviceIdType.MESH,
        )
        copies.append(copy)
    for slot in (3, 4, 2, 0, 1):
        pl.when(present(*sends[slot]))(copies[slot].start)

    for slot, (seq_step, slab_step) in enumerate(sends):
        pl.when(present(-seq_step, -slab_step))(copies[slot].wait_recv)

    lane = lax.broadcasted_iota(jnp.int32, (token_cols, LANES), 1)
    line = lax.broadcasted_iota(jnp.int32, (token_cols, LANES), 0)
    odd = lax.rem(lax.div(lane, chan), 2) == 1

    def turned(value, amount):
        return pltpu.roll(value, amount % LANES, 1) if amount % LANES else value

    columns_of = []
    for center_block, above, below in (
        (halo_buf[2].astype(F32), halo_buf[3].astype(F32), halo_buf[4].astype(F32)),
        (latent.astype(F32), halo_buf[0].astype(F32), halo_buf[1].astype(F32)),
    ):
        for f in range(frames):
            base = f * 2 * span
            full = turned(center_block, span - base)
            full = jnp.where(lane < span, turned(above, -base - span), full)
            full = jnp.where(lane >= 3 * span, turned(below, 3 * span - base), full)
            before = jnp.where(line == 0, 0.0, pltpu.roll(full, 1, 0))
            after = jnp.where(line == token_cols - 1, 0.0, pltpu.roll(full, token_cols - 1, 0))
            beside = jnp.where(odd, before, after)
            lower = (turned(full, -span), turned(beside, -span))
            columns_of.append(
                (
                    (full.astype(BF16), beside.astype(BF16)),
                    (lower[0].astype(BF16), lower[1].astype(BF16)),
                )
            )
    taps = taps_buf[...]
    bias = conv_bias_buf[...]
    columns = jnp.concatenate(
        [
            jnp.concatenate(
                [piece for t in range(3) for piece in columns_of[f + t][y]], axis=1
            )
            for f in range(frames)
            for y in range(2)
        ],
        axis=0,
    )
    result = dot_nn(columns, taps)
    for f in range(frames):
        for y in range(2):
            first = (f * 2 + y) * token_cols
            for part in range(out_chan // LANES):
                lanes = slice(part * LANES, (part + 1) * LANES)
                for e in range(2):
                    from_lane = e * out_chan + part * LANES
                    wide_buf[part, pl.ds(2 * first + e, token_cols, stride=2), :] = (
                        result[first : first + token_cols, from_lane : from_lane + LANES]
                        + bias[:, lanes]
                    )
                out_ref[f, y, :, lanes] = wide_buf[
                    part, 2 * first : 2 * first + 2 * token_cols, :
                ].astype(BF16)

    pair.wait_send()
    for slot in range(len(sends)):
        pl.when(present(*sends[slot]))(copies[slot].wait_send)


def per_device(
    counts,
    hidden,
    token_order,
    noisy_latent,
    head_weight,
    head_mod,
    guidance,
    timestep_index,
    step_table,
    vae_mean,
    vae_std,
    conv2_weight,
    conv2_bias,
    conv1_weight,
    conv1_bias,
):
    frames, lat_rows, lat_width = noisy_latent.shape
    chan = vae_mean.shape[0]
    tokens, width = hidden.shape[1:]
    patch = head_weight.shape[1]
    out_chan = conv1_weight.shape[2]
    token_cols = lat_width // (2 * chan)
    token_rows = lat_rows * counts[2] // 2
    chunks = 5
    operands = (
        hidden,
        token_order.reshape(1, -1),
        noisy_latent.reshape(frames, lat_rows, lat_width // LANES, LANES),
        head_weight.T,
        head_mod,
        guidance.reshape(1, 1),
        timestep_index.reshape(1, 1),
        step_table.reshape(1, -1),
        vae_mean.reshape(1, -1),
        vae_std.reshape(1, -1),
        conv2_weight,
        conv2_bias.reshape(1, -1),
        conv1_weight,
        conv1_bias.reshape(1, -1),
    )
    block = (token_cols, LANES)
    scratch = [
        pltpu.VMEM((tokens + EXTRA, width), BF16),
        pltpu.VMEM((patch, width), BF16),
        pltpu.VMEM((2 * patch + EXTRA, width), BF16),
        pltpu.VMEM(operands[1].shape, jnp.int32),
        pltpu.VMEM(operands[2].shape, F32),
    ]
    scratch += [pltpu.VMEM(value.shape, value.dtype) for value in operands[4:]]
    scratch += [
        pltpu.VMEM(block, F32),
        pltpu.VMEM((3 * 16 * chan, 2 * out_chan), BF16),
        pltpu.VMEM((token_rows,) + block, F32),
        pltpu.VMEM(block, F32),
        pltpu.VMEM(block, BF16),
        pltpu.VMEM((5,) + block, BF16),
        pltpu.VMEM((out_chan // LANES, frames * lat_rows * 2 * token_cols, LANES), F32),
        pltpu.SemaphoreType.DMA((12,)),
        pltpu.SemaphoreType.DMA((2, chunks)),
        pltpu.SemaphoreType.DMA((6,)),
        pltpu.SemaphoreType.DMA((6,)),
    ]
    sizes = tuple(counts) + (token_rows, token_cols, frames, chunks)
    return pl.pallas_call(
        functools.partial(kernel, sizes),
        out_shape=jax.ShapeDtypeStruct((frames, lat_rows, 2 * token_cols, out_chan), BF16),
        in_specs=[pl.BlockSpec(memory_space=pl.ANY)] * len(operands),
        out_specs=pl.BlockSpec(memory_space=pltpu.VMEM),
        scratch_shapes=scratch,
        compiler_params=pltpu.CompilerParams(
            collective_id=0, has_side_effects=True, vmem_limit_bytes=60 * 1024 * 1024
        ),
        name="guided_step",
    )(*operands)


def solution(mesh):
    counts = (mesh.shape["seq"], mesh.shape["rows"], mesh.shape["cfg"])
    return jax.shard_map(
        functools.partial(per_device, counts),
        mesh=mesh,
        in_specs=(
            P("cfg", ("groups", "seq", "rows"), None),
            P(("groups", "seq", "rows")),
            P(("groups", "seq"), ("rows", "cfg"), None),
            P(),
            P(),
            P(),
            P(),
            P(),
            P(),
            P(),
            P(),
            P(),
            P(),
            P(),
        ),
        out_specs=P(("groups", "seq"), ("rows", "cfg"), None, None),
        check_vma=False,
    )
```

time: 36.6 us -> 17.2 us (0.47)
  Pallas kernels: 0 us -> 11.1 us
  starting transfers between devices: 9.63 us -> 0 us
  local copies, waits for them, and re-layouts: 9.76 us -> 4.44 us
  waiting for transfers between devices: 4.13 us -> 0 us
  other arithmetic: 4.12 us -> 0 us
  matrix products: 3.55 us -> 0 us
  blocking collectives: 1.9 us -> 0 us
  between operations: 2.99 us -> 1.31 us
    pallas_call x0 -> x1, Pallas kernels: none -> 11.1 us  [per_device(): pl.pallas_call(functools.partial(kernel, sizes), out_shape=jax.ShapeDtype...]
    ppermute x3 -> x0, starting transfers between devices: 9.63 us -> none  [the longest x1 4.51 us: padded_2(): lax.ppermute(lax.slice_in_dim(block, block.shape[dim] - width, None, axis...]
    ppermute x3 -> x0, waiting for transfers between devices: 4.13 us -> none  [the longest x1 3.12 us: padded_2(): lax.ppermute(lax.slice_in_dim(block, 0, width, axis=dim), axis, backward)]
    dot_general x3 -> x0, matrix products: 3.55 us -> none  [the longest x1 2.16 us: per_device(): jnp.dot(tap_columns, kernel, preferred_element_type=jnp.float32)]
    reduce_sum x2 -> x0, other arithmetic: 3.01 us -> none  [the longest x1 2.18 us: head_rows(): center = jnp.mean(values, axis=-1, keepdims=True)]
    concatenate x1 -> x0, local copies, waits for them, and re-layouts: 2.88 us -> none  [conv_taps(): return jnp.concatenate(pieces, axis=-1)]
    slice x5 -> x0, local copies, waits for them, and re-layouts: 2.2 us -> none  [the longest x3 2.17 us: conv_taps(): padded[step_time:step_time + frames, step_row:step_row + row_count, step_...]
    all_gather x1 -> x0, blocking collectives: 1.9 us -> none  [per_device(): gathered = lax.all_gather(local_block[None], 'cfg', axis=0, tiled=True)]
  transfers between devices with their start and end apart: 3 -> 0, of which waited for: 2 -> 0; matrix products, arithmetic and copies ran while one was open for 0% -> 0% of each run, Pallas kernels for 0% -> 0%
where the time goes in v1:
time: 17.2 us; the launch traced here: 16.9 us
  Pallas kernels  11.1 us (65%)
  local copies, waits for them, and re-layouts  4.44 us (26%)
  between operations  1.31 us (8%)
    pallas_call x1, Pallas kernels, per_device(): pl.pallas_call(functools.partial(kernel, sizes), out_shape=jax.ShapeDtype...  11.1 us
    unnamed x1, local copies, waits for them, and re-layouts  1.78 us
    reshape x1, local copies, waits for them, and re-layouts, per_device(): noisy_latent.reshape(frames, lat_rows, lat_width // LANES, LANES)  1.4 us
    reshape x1, local copies, waits for them, and re-layouts, per_device(): conv1_bias.reshape(1, -1)  1.26 us

profile of v1, /device:TPU:1, one launch (start us, length us, event | category | flops | bytes accessed | tf_op | source)
XLA Modules:
  0.0 16.9 jit_solution(3771551541729885456)
XLA Ops:
  1.3 1.3 %reshape.35.conv_bias_hbm = f32[1,384]{1,0:T(1,128)} reshape(f32[384]{0:T(512)} %param.27) | data formatting | bytes 3072 | tf_op jit(solution)/shard_map/reshape | solution.py:432
  2.6 1.4 %reshape.28.noisy_hbm = f32[2,2,16,128]{3,2,1,0:T(8,128)} reshape(f32[2,2,2048]{2,1,0:T(2,128)} %param.16) | data formatting | bytes 65536 | tf_op jit(solution)/shard_map/reshape | solution.py:421
  4.0 11.1 %guided_step.1 = bf16[2,2,128,384]{3,2,1,0:T(8,128)(2,1)} custom-call(bf16[1,256,5120]{2,1,0:T(8,128)(2,1)} %hidden_hbm.1, s32[1,256]{1,0:T(1,128)} %bitcast.11, f32[2,2,16,128]{3,2,1,0:T(8,128)} %reshape.28.noisy_hbm, bf16[64,5120]{1,0:T(8,128)(2,1)} %bitcast.10, f32[2,5120]{1,0:T(2,128)} %mod_hbm.1, f32[1,1]{1,0:T(1,128)} %bitcast.8.guidance_hbm, ...), custom_call_target="tpu_custom_call" | custom-call | tf_op jit(solution)/shard_map/guided_step/pallas_call | solution.py:457
  15.1 1.8 %copy.18 = bf16[2,2,128,384]{3,2,1,0:T(8,128)(2,1)} copy(bf16[2,2,128,384]{3,2,1,0:T(8,128)(2,1)} %guided_step.1) | data formatting | bytes 786432

commit v2 on v1

--- a/solution.py
+++ b/solution.py
@@ -34,9 +34,9 @@
     noisy_hbm,
     weight_hbm,
     mod_hbm,
-    guidance_hbm,
-    index_hbm,
-    table_hbm,
+    guidance_ref,
+    index_ref,
+    table_ref,
     mean_hbm,
     std_hbm,
     mix_hbm,
@@ -50,15 +50,13 @@
     order_buf,
     noisy_buf,
     mod_buf,
-    guidance_buf,
-    index_buf,
-    table_buf,
     mean_buf,
     std_buf,
     mix_buf,
     mix_bias_buf,
     conv_buf,
     conv_bias_buf,
+    lines_buf,
     latent_buf,
     taps_buf,
     cells_buf,
@@ -90,9 +88,6 @@
         (mod_hbm, mod_buf),
         (order_hbm, order_buf),
         (noisy_hbm, noisy_buf),
-        (guidance_hbm, guidance_buf),
-        (index_hbm, index_buf),
-        (table_hbm, table_buf),
         (mean_hbm, mean_buf),
         (std_hbm, std_buf),
         (mix_hbm, mix_buf),
@@ -117,11 +112,13 @@
             )
         )
     small[0].start()
-    for weight_copy, hidden_copy in loads:
+    for index, (weight_copy, hidden_copy) in enumerate(loads):
         weight_copy.start()
         hidden_copy.start()
-    for copy in small[1:]:
-        copy.start()
+        if index == 0:
+            for copy in small[1:-1]:
+                copy.start()
+    small[-1].start()
 
     barrier = pltpu.get_barrier_semaphore()
 
@@ -168,6 +165,58 @@
     ).astype(BF16)
     ones_row = lax.broadcasted_iota(jnp.int32, (EXTRA, width), 0) == 0
     rhs_buf[2 * patch : 2 * patch + EXTRA, :] = jnp.where(ones_row, 1.0, 0.0).astype(BF16)
+
+    for copy in small[1:-1]:
+        copy.wait()
+    cell = order_buf[...].astype(F32) + 0.5
+    per_frame = float(row_count * token_rows * token_cols)
+    frame_all = jnp.floor(cell * (1.0 / per_frame))
+    in_frame = cell - frame_all * per_frame
+    frame_pos = frame_all - frames * jnp.floor((frame_all + 0.5) * (1.0 / frames))
+    row_all = jnp.floor(in_frame * (1.0 / token_cols))
+    column = in_frame - 0.5 - row_all * token_cols
+    row_pos = row_all - token_rows * jnp.floor((row_all + 0.5) * (1.0 / token_rows))
+    target = (frame_pos * token_rows + row_pos) * token_cols + column
+    wanted = lax.broadcasted_iota(jnp.int32, (tokens, tokens), 0).astype(F32)
+    one_hot = jnp.where(jnp.abs(wanted - target) < 0.25, 1.0, 0.0).astype(BF16)
+    for f in range(frames):
+        for a in range(2):
+            for g in range(lines_buf.shape[2]):
+                lines_buf[f, a, g : g + 1, :] = noisy_buf[f, a : a + 1, g * LANES : (g + 1) * LANES]
+    lane = lax.broadcasted_iota(jnp.int32, (lines_buf.shape[2], LANES), 1)
+    span = 2 * chan
+    per_line = LANES // span
+    groups = lines_buf.shape[2]
+    for jj in range(per_line):
+        line = jnp.zeros((groups, LANES), F32)
+        for f in range(frames):
+            for a in range(2):
+                slot = f * 2 + a
+                moved = lines_buf[f, a]
+                if (slot - jj) % per_line:
+                    moved = pltpu.roll(moved, ((slot - jj) * span) % LANES, 1)
+                line = jnp.where((lane >= slot * span) & (lane < (slot + 1) * span), moved, line)
+        latent_buf[pl.ds(jj, groups, stride=per_line), :] = line
+
+    repeat = LANES // chan
+
+    def lanes_of(ref):
+        return jnp.concatenate([ref[...]] * repeat, axis=1)
+
+    mean_row = lanes_of(mean_buf)
+    std_row = lanes_of(std_buf)
+    mix_row = lanes_of(mix_bias_buf)
+    mix = jnp.concatenate([lanes_of(mix_buf)] * repeat, axis=0)
+    mix_in = lax.broadcasted_iota(jnp.int32, (LANES, LANES), 0)
+    mix_out = lax.broadcasted_iota(jnp.int32, (LANES, LANES), 1)
+    same = lax.div(mix_in, chan) == lax.div(mix_out, chan)
+    mix_high, mix_low = split_bf16(jnp.where(same, mix, 0.0))
+    mix_both = jnp.concatenate([mix_high, mix_low], axis=1)
+
+    at = index_ref[0]
+    now = jnp.full((1, LANES), table_ref[at].astype(F32))
+    later = jnp.full((1, LANES), table_ref[at + 1].astype(F32))
+    step_size = later / 1000.0 - now / 1000.0
 
     block = 64
     blocks = tokens // block
@@ -208,19 +257,6 @@
     offset_row = both[:, patch : 2 * patch]
     head = (product[0:tokens, 0:patch] - average * column_sum) * inverse + offset_row
 
-    for copy in small[1:]:
-        copy.wait()
-    cell = order_buf[...].astype(F32) + 0.5
-    per_frame = float(row_count * token_rows * token_cols)
-    frame_all = jnp.floor(cell * (1.0 / per_frame))
-    in_frame = cell - frame_all * per_frame
-    frame_pos = frame_all - frames * jnp.floor((frame_all + 0.5) * (1.0 / frames))
-    row_all = jnp.floor(in_frame * (1.0 / token_cols))
-    column = in_frame - 0.5 - row_all * token_cols
-    row_pos = row_all - token_rows * jnp.floor((row_all + 0.5) * (1.0 / token_rows))
-    target = (frame_pos * token_rows + row_pos) * token_cols + column
-    wanted = lax.broadcasted_iota(jnp.int32, (tokens, tokens), 0).astype(F32)
-    one_hot = jnp.where(jnp.abs(wanted - target) < 0.25, 1.0, 0.0).astype(BF16)
     head_high, head_low = split_bf16(head)
     placed = dot_nn(one_hot, head_high) + dot_nn(one_hot, head_low)
     per = token_rows * token_cols
@@ -245,42 +281,7 @@
     )
     pair.start()
 
-    lane = lax.broadcasted_iota(jnp.int32, (noisy_buf.shape[2], LANES), 1)
-    span = 2 * chan
-    per_line = LANES // span
-    groups = noisy_buf.shape[2]
-    for jj in range(per_line):
-        line = jnp.zeros((groups, LANES), F32)
-        for f in range(frames):
-            for a in range(2):
-                slot = f * 2 + a
-                moved = noisy_buf[f, a]
-                if (slot - jj) % per_line:
-                    moved = pltpu.roll(moved, ((slot - jj) * span) % LANES, 1)
-                line = jnp.where((lane >= slot * span) & (lane < (slot + 1) * span), moved, line)
-        latent_buf[pl.ds(jj, groups, stride=per_line), :] = line
-
-    repeat = LANES // chan
-
-    def lanes_of(ref):
-        return jnp.concatenate([ref[...]] * repeat, axis=1)
-
-    mean_row = lanes_of(mean_buf)
-    std_row = lanes_of(std_buf)
-    mix_row = lanes_of(mix_bias_buf)
-    mix = jnp.concatenate([lanes_of(mix_buf)] * repeat, axis=0)
-    mix_in = lax.broadcasted_iota(jnp.int32, (LANES, LANES), 0)
-    mix_out = lax.broadcasted_iota(jnp.int32, (LANES, LANES), 1)
-    same = lax.div(mix_in, chan) == lax.div(mix_out, chan)
-    mix_high, mix_low = split_bf16(jnp.where(same, mix, 0.0))
-    mix_both = jnp.concatenate([mix_high, mix_low], axis=1)
-
-    spot = lax.broadcasted_iota(jnp.int32, table_buf.shape, 1)
-    table = table_buf[...].astype(F32)
-    now = jnp.sum(jnp.where(spot == index_buf[...], table, 0.0), axis=1, keepdims=True)
-    later = jnp.sum(jnp.where(spot == index_buf[...] + 1, table, 0.0), axis=1, keepdims=True)
-    step_size = later / 1000.0 - now / 1000.0
-
+    small[-1].wait()
     position = 0
     for t in range(3):
         for shifted in range(2):
@@ -302,7 +303,7 @@
     partner = partner_buf[...]
     cond = jnp.where(half == 0, own, partner)
     free = jnp.where(half == 0, partner, own)
-    velocity = free + guidance_buf[...] * (cond - free)
+    velocity = free + guidance_ref[0] * (cond - free)
     stepped = latent_buf[...] + step_size * velocity
     channels = stepped * std_row + mean_row
     high, low = split_bf16(channels)
@@ -379,7 +380,7 @@
                     from_lane = e * out_chan + part * LANES
                     wide_buf[part, pl.ds(2 * first + e, token_cols, stride=2), :] = (
                         result[first : first + token_cols, from_lane : from_lane + LANES]
-                        + bias[:, lanes]
+                        + bias[part : part + 1, :]
                     )
                 out_ref[f, y, :, lanes] = wide_buf[
                     part, 2 * first : 2 * first + 2 * token_cols, :
@@ -418,18 +419,18 @@
     operands = (
         hidden,
         token_order.reshape(1, -1),
-        noisy_latent.reshape(frames, lat_rows, lat_width // LANES, LANES),
+        noisy_latent,
         head_weight.T,
         head_mod,
-        guidance.reshape(1, 1),
-        timestep_index.reshape(1, 1),
-        step_table.reshape(1, -1),
+        guidance,
+        timestep_index,
+        step_table,
         vae_mean.reshape(1, -1),
         vae_std.reshape(1, -1),
         conv2_weight,
         conv2_bias.reshape(1, -1),
         conv1_weight,
-        conv1_bias.reshape(1, -1),
+        conv1_bias.reshape(-1, LANES),
     )
     block = (token_cols, LANES)
     scratch = [
@@ -439,8 +440,13 @@
         pltpu.VMEM(operands[1].shape, jnp.int32),
         pltpu.VMEM(operands[2].shape, F32),
     ]
-    scratch += [pltpu.VMEM(value.shape, value.dtype) for value in operands[4:]]
     scratch += [
+        pltpu.VMEM(value.shape, value.dtype)
+        for index, value in enumerate(operands)
+        if index == 4 or index > 7
+    ]
+    scratch += [
+        pltpu.VMEM((frames, lat_rows, lat_width // LANES, LANES), F32),
         pltpu.VMEM(block, F32),
         pltpu.VMEM((3 * 16 * chan, 2 * out_chan), BF16),
         pltpu.VMEM((token_rows,) + block, F32),
@@ -448,7 +454,7 @@
         pltpu.VMEM(block, BF16),
         pltpu.VMEM((5,) + block, BF16),
         pltpu.VMEM((out_chan // LANES, frames * lat_rows * 2 * token_cols, LANES), F32),
-        pltpu.SemaphoreType.DMA((12,)),
+        pltpu.SemaphoreType.DMA((9,)),
         pltpu.SemaphoreType.DMA((2, chunks)),
         pltpu.SemaphoreType.DMA((6,)),
         pltpu.SemaphoreType.DMA((6,)),
@@ -456,15 +462,25 @@
     sizes = tuple(counts) + (token_rows, token_cols, frames, chunks)
     return pl.pallas_call(
         functools.partial(kernel, sizes),
-        out_shape=jax.ShapeDtypeStruct((frames, lat_rows, 2 * token_cols, out_chan), BF16),
-        in_specs=[pl.BlockSpec(memory_space=pl.ANY)] * len(operands),
+        out_shape=pltpu.VMEM((frames, lat_rows, 2 * token_cols, out_chan), BF16),
+        in_specs=[
+            pl.BlockSpec(memory_space=pltpu.SMEM if index in (5, 6, 7) else pl.ANY)
+            for index in range(len(operands))
+        ],
         out_specs=pl.BlockSpec(memory_space=pltpu.VMEM),
         scratch_shapes=scratch,
         compiler_params=pltpu.CompilerParams(
             collective_id=0, has_side_effects=True, vmem_limit_bytes=60 * 1024 * 1024
         ),
         name="guided_step",
-    )(*operands)
+    )(
+        *[
+            value
+            if index in (5, 6, 7)
+            else pltpu.with_memory_space_constraint(value, pltpu.HBM)
+            for index, value in enumerate(operands)
+        ]
+    )
 
 
 def solution(mesh):

time: 17.2 us -> 13.4 us (0.78); the launches traced: 16.9 us -> 13.3 us
  local copies, waits for them, and re-layouts: 4.44 us -> 0.75 us
    reshape x2 -> x0, local copies, waits for them, and re-layouts: 2.66 us -> none  [the longest x1 1.4 us: per_device(): noisy_latent.reshape(frames, lat_rows, lat_width // LANES, LANES)]
    unnamed x1, local copies, waits for them, and re-layouts: 1.78 us -> 0.75 us
where the time goes in v2:
time: 13.4 us; the launch traced here: 13.3 us
  Pallas kernels  11.2 us (84%)
  between operations  1.3 us (10%)
  local copies, waits for them, and re-layouts  0.75 us (6%)
    pallas_call x1, Pallas kernels, per_device(): pl.pallas_call(functools.partial(kernel, sizes), out_shape=pltpu.VMEM((fr...  11.2 us
    unnamed x1, local copies, waits for them, and re-layouts  0.75 us

profile of v2, /device:TPU:1, one launch (start us, length us, event | category | flops | bytes accessed | tf_op | source)
XLA Modules:
  0.0 13.3 jit_solution(720994672812725570)
XLA Ops:
  1.3 11.2 %guided_step.1 = bf16[2,2,128,384]{3,2,1,0:T(8,128)(2,1)S(1)} custom-call(bf16[1,256,5120]{2,1,0:T(8,128)(2,1)} %hidden_hbm.1, s32[1,256]{1,0:T(1,128)} %bitcast.8, f32[2,2,2048]{2,1,0:T(2,128)} %noisy_hbm.1, bf16[64,5120]{1,0:T(8,128)(2,1)} %bitcast.6, f32[2,5120]{1,0:T(2,128)} %mod_hbm.1, f32[1]{0:T(128)S(6)} %copy.17.guidance_ref, s32[1]{0:T(128)S(6)} %copy.18.index_ref, ...), custom_call_target="tpu_custom_call" | custom-call | tf_op jit(solution)/shard_map/guided_step/pallas_call | solution.py:463
  12.5 0.7 %copy.16 = bf16[2,2,128,384]{3,2,1,0:T(8,128)(2,1)} copy(bf16[2,2,128,384]{3,2,1,0:T(8,128)(2,1)S(1)} %guided_step.1) | data formatting | bytes 786432

commit v3 on v2

--- a/solution.py
+++ b/solution.py
@@ -61,6 +61,7 @@
     taps_buf,
     cells_buf,
     partner_buf,
+    center_buf,
     edge_buf,
     halo_buf,
     wide_buf,
@@ -97,27 +98,23 @@
     ):
         small.append(pltpu.make_async_copy(source, target, local_sem.at[len(small)]))
     loads = []
+    weight_copy = pltpu.make_async_copy(weight_hbm, w_buf, chunk_sem.at[0])
     for part in range(chunks):
         columns = pl.ds(part * step, step)
         loads.append(
-            (
-                pltpu.make_async_copy(
-                    weight_hbm.at[:, columns], w_buf.at[:, columns], chunk_sem.at[0, part]
-                ),
-                pltpu.make_async_copy(
-                    hidden_hbm.at[0, :, columns],
-                    x_buf.at[pl.ds(0, tokens), columns],
-                    chunk_sem.at[1, part],
-                ),
+            pltpu.make_async_copy(
+                hidden_hbm.at[0, :, columns],
+                x_buf.at[pl.ds(0, tokens), columns],
+                chunk_sem.at[1 + part],
             )
         )
     small[0].start()
-    for index, (weight_copy, hidden_copy) in enumerate(loads):
-        weight_copy.start()
-        hidden_copy.start()
-        if index == 0:
-            for copy in small[1:-1]:
-                copy.start()
+    weight_copy.start()
+    loads[0].start()
+    for copy in small[1:-1]:
+        copy.start()
+    for copy in loads[1:]:
+        copy.start()
     small[-1].start()
 
     barrier = pltpu.get_barrier_semaphore()
@@ -152,7 +149,10 @@
 
         @pl.when(jnp.logical_not(present(-seq_step, -slab_step)))
         def _(slot=slot):
-            halo_buf[slot] = jnp.zeros(halo_buf.shape[1:], BF16)
+            if sends[slot][1]:
+                halo_buf[slot] = jnp.zeros(halo_buf.shape[1:], BF16)
+            else:
+                center_buf[1] = jnp.zeros(center_buf.shape[1:], BF16)
 
     small[0].wait()
     scale = 1.0 + mod_buf[1:2, :]
@@ -209,7 +209,13 @@
     mix = jnp.concatenate([lanes_of(mix_buf)] * repeat, axis=0)
     mix_in = lax.broadcasted_iota(jnp.int32, (LANES, LANES), 0)
     mix_out = lax.broadcasted_iota(jnp.int32, (LANES, LANES), 1)
-    same = lax.div(mix_in, chan) == lax.div(mix_out, chan)
+    group_in = lax.div(mix_in, chan)
+    wanted_out = (
+        lax.rem(lax.div(group_in, 2), 2) * (2 * frames)
+        + lax.div(group_in, 4) * 2
+        + lax.rem(group_in, 2)
+    )
+    same = wanted_out == lax.div(mix_out, chan)
     mix_high, mix_low = split_bf16(jnp.where(same, mix, 0.0))
     mix_both = jnp.concatenate([mix_high, mix_low], axis=1)
 
@@ -217,20 +223,18 @@
     now = jnp.full((1, LANES), table_ref[at].astype(F32))
     later = jnp.full((1, LANES), table_ref[at + 1].astype(F32))
     step_size = later / 1000.0 - now / 1000.0
+
+    weight_copy.wait()
+    rhs_buf[0:patch, :] = (w_buf[...].astype(F32) * scale).astype(BF16)
+    rhs_buf[patch : 2 * patch, :] = w_buf[...]
 
     block = 64
     blocks = tokens // block
     product = jnp.zeros((tokens + EXTRA, rhs_buf.shape[0]), F32)
     centers = [None] * blocks
     squares = [jnp.zeros((block, LANES), F32)] * blocks
-    for part, (weight_copy, hidden_copy) in enumerate(loads):
+    for part, hidden_copy in enumerate(loads):
         low = part * step
-        weight_copy.wait()
-        raw = w_buf[:, low : low + step]
-        rhs_buf[0:patch, low : low + step] = (
-            raw.astype(F32) * scale[:, low : low + step]
-        ).astype(BF16)
-        rhs_buf[patch : 2 * patch, low : low + step] = raw
         hidden_copy.wait()
         product = product + dot_nt(x_buf[:, low : low + step], rhs_buf[:, low : low + step])
         for index in range(blocks):
@@ -312,13 +316,23 @@
         mixed[0:token_cols, LANES:] + mixed[token_cols:, 0:LANES]
     )
     latent = (mixed + mix_row).astype(BF16)
-    edge_buf[...] = latent
+    exact = latent.astype(F32)
+    fold = token_cols // 2
+    left = lax.broadcasted_iota(jnp.int32, (fold, LANES), 1) < LANES // 2
+    first, second = exact[0:fold], exact[fold:]
+    edge_buf[0] = jnp.where(left, first, pltpu.roll(second, LANES // 2, 1)).astype(BF16)
+    edge_buf[1] = jnp.where(left, pltpu.roll(first, LANES // 2, 1), second).astype(BF16)
+    center_buf[0] = latent
 
     copies = []
     for slot, (seq_step, slab_step) in enumerate(sends):
+        if slab_step:
+            source, target = edge_buf.at[(1 + slab_step) // 2], halo_buf.at[slot]
+        else:
+            source, target = center_buf.at[0], center_buf.at[1]
         copy = pltpu.make_async_remote_copy(
-            src_ref=edge_buf,
-            dst_ref=halo_buf.at[slot],
+            src_ref=source,
+            dst_ref=target,
             send_sem=send_sem.at[1 + slot],
             recv_sem=recv_sem.at[1 + slot],
             device_id=place(seq_step, slab_step),
@@ -338,16 +352,21 @@
     def turned(value, amount):
         return pltpu.roll(value, amount % LANES, 1) if amount % LANES else value
 
+    def spread_rows(block, f, lane_base):
+        return jnp.concatenate(
+            [turned(block, lane_base - (part * frames + f) * span) for part in range(2)], axis=0
+        )
+
     columns_of = []
     for center_block, above, below in (
-        (halo_buf[2].astype(F32), halo_buf[3].astype(F32), halo_buf[4].astype(F32)),
-        (latent.astype(F32), halo_buf[0].astype(F32), halo_buf[1].astype(F32)),
+        (center_buf[1].astype(F32), halo_buf[3].astype(F32), halo_buf[4].astype(F32)),
+        (exact, halo_buf[0].astype(F32), halo_buf[1].astype(F32)),
     ):
         for f in range(frames):
-            base = f * 2 * span
-            full = turned(center_block, span - base)
-            full = jnp.where(lane < span, turned(above, -base - span), full)
-            full = jnp.where(lane >= 3 * span, turned(below, 3 * span - base), full)
+            full = turned(center_block, span - f * span)
+            full = jnp.where(lane >= 2 * span, turned(center_block, -f * span), full)
+            full = jnp.where(lane < span, spread_rows(above, f, 0), full)
+            full = jnp.where(lane >= 3 * span, spread_rows(below, f, 3 * span), full)
             before = jnp.where(line == 0, 0.0, pltpu.roll(full, 1, 0))
             after = jnp.where(line == token_cols - 1, 0.0, pltpu.roll(full, token_cols - 1, 0))
             beside = jnp.where(odd, before, after)
@@ -451,11 +470,12 @@
         pltpu.VMEM((3 * 16 * chan, 2 * out_chan), BF16),
         pltpu.VMEM((token_rows,) + block, F32),
         pltpu.VMEM(block, F32),
-        pltpu.VMEM(block, BF16),
-        pltpu.VMEM((5,) + block, BF16),
+        pltpu.VMEM((2,) + block, BF16),
+        pltpu.VMEM((2, token_cols // 2, LANES), BF16),
+        pltpu.VMEM((5, token_cols // 2, LANES), BF16),
         pltpu.VMEM((out_chan // LANES, frames * lat_rows * 2 * token_cols, LANES), F32),
         pltpu.SemaphoreType.DMA((9,)),
-        pltpu.SemaphoreType.DMA((2, chunks)),
+        pltpu.SemaphoreType.DMA((1 + chunks,)),
         pltpu.SemaphoreType.DMA((6,)),
         pltpu.SemaphoreType.DMA((6,)),
     ]

time: 13.4 us -> 13.3 us (level)
  no operation moved by 1% of the time
where the time goes in v3:
time: 13.3 us; the launch traced here: 13.2 us
  Pallas kernels  11.1 us (83%)
  between operations  1.3 us (10%)
  local copies, waits for them, and re-layouts  0.75 us (6%)
    pallas_call x1, Pallas kernels, per_device(): pl.pallas_call(functools.partial(kernel, sizes), out_shape=pltpu.VMEM((fr...  11.1 us
    unnamed x1, local copies, waits for them, and re-layouts  0.75 us

profile of v3, /device:TPU:1, one launch (start us, length us, event | category | flops | bytes accessed | tf_op | source)
XLA Modules:
  0.0 13.2 jit_solution(7829748330564940317)
XLA Ops:
  1.3 11.1 %guided_step.1 = bf16[2,2,128,384]{3,2,1,0:T(8,128)(2,1)S(1)} custom-call(bf16[1,256,5120]{2,1,0:T(8,128)(2,1)} %hidden_hbm.1, s32[1,256]{1,0:T(1,128)} %bitcast.8, f32[2,2,2048]{2,1,0:T(2,128)} %noisy_hbm.1, bf16[64,5120]{1,0:T(8,128)(2,1)} %bitcast.6, f32[2,5120]{1,0:T(2,128)} %mod_hbm.1, f32[1]{0:T(128)S(6)} %copy.17.guidance_ref, s32[1]{0:T(128)S(6)} %copy.18.index_ref, ...), custom_call_target="tpu_custom_call" | custom-call | tf_op jit(solution)/shard_map/guided_step/pallas_call | solution.py:483
  12.4 0.7 %copy.16 = bf16[2,2,128,384]{3,2,1,0:T(8,128)(2,1)} copy(bf16[2,2,128,384]{3,2,1,0:T(8,128)(2,1)S(1)} %guided_step.1) | data formatting | bytes 786432

commit v4 on v3

--- a/solution.py
+++ b/solution.py
@@ -104,7 +104,7 @@
         loads.append(
             pltpu.make_async_copy(
                 hidden_hbm.at[0, :, columns],
-                x_buf.at[pl.ds(0, tokens), columns],
+                x_buf.at[:, columns],
                 chunk_sem.at[1 + part],
             )
         )
@@ -156,15 +156,8 @@
 
     small[0].wait()
     scale = 1.0 + mod_buf[1:2, :]
-    shift_high, shift_low = split_bf16(mod_buf[0:1, :])
-    pick = lax.broadcasted_iota(jnp.int32, (EXTRA, width), 0)
-    x_buf[tokens : tokens + EXTRA, :] = jnp.where(
-        pick == 0,
-        shift_high.astype(F32),
-        jnp.where(pick == 1, shift_low.astype(F32), jnp.where(pick == 2, 1.0, 0.0)),
-    ).astype(BF16)
     ones_row = lax.broadcasted_iota(jnp.int32, (EXTRA, width), 0) == 0
-    rhs_buf[2 * patch : 2 * patch + EXTRA, :] = jnp.where(ones_row, 1.0, 0.0).astype(BF16)
+    rhs_buf[patch : patch + EXTRA, :] = jnp.where(ones_row, 1.0, 0.0).astype(BF16)
 
     for copy in small[1:-1]:
         copy.wait()
@@ -179,6 +172,79 @@
     target = (frame_pos * token_rows + row_pos) * token_cols + column
     wanted = lax.broadcasted_iota(jnp.int32, (tokens, tokens), 0).astype(F32)
     one_hot = jnp.where(jnp.abs(wanted - target) < 0.25, 1.0, 0.0).astype(BF16)
+    weight_copy.wait()
+    column_part = jnp.zeros((patch, LANES), F32)
+    offset_part = jnp.zeros((patch, LANES), F32)
+    for lane in range(0, width, LANES):
+        lanes = slice(lane, lane + LANES)
+        raw = w_buf[:, lanes].astype(F32)
+        scaled = (raw * scale[:, lanes]).astype(BF16)
+        rhs_buf[0:patch, lanes] = scaled
+        column_part = column_part + scaled.astype(F32)
+        offset_part = offset_part + raw * mod_buf[0:1, lanes]
+    rest = jnp.concatenate([column_part, offset_part], axis=0)
+    ones = jnp.ones((EXTRA, LANES), BF16)
+    sums = jnp.zeros((EXTRA, 2 * patch), F32)
+    for _ in range(3):
+        piece = rest.astype(BF16)
+        rest = rest - piece.astype(F32)
+        sums = sums + dot_nt(ones, piece)
+    column_sum = sums[0:1, 0:patch]
+    offset_row = sums[0:1, patch:]
+
+    block = 64
+    blocks = tokens // block
+    product = jnp.zeros((tokens, rhs_buf.shape[0]), F32)
+    centers = [None] * blocks
+    squares = [jnp.zeros((block, LANES), F32)] * blocks
+    for part, hidden_copy in enumerate(loads):
+        low = part * step
+        hidden_copy.wait()
+        product = product + dot_nt(x_buf[:, low : low + step], rhs_buf[:, low : low + step])
+        for index in range(blocks):
+            rows = slice(index * block, (index + 1) * block)
+            if part == 0:
+                total = x_buf[rows, 0:LANES].astype(F32)
+                center = jnp.sum(total, axis=1, keepdims=True) * (1.0 / LANES)
+                centers[index] = jnp.broadcast_to(center, (block, LANES))
+            square = squares[index]
+            for lane in range(low, low + step, LANES):
+                gap = x_buf[rows, lane : lane + LANES].astype(F32) - centers[index]
+                square = square + gap * gap
+            squares[index] = square
+
+    center = jnp.concatenate([value[:, 0:1] for value in centers], axis=0)
+    spread = jnp.concatenate([jnp.sum(value, axis=1, keepdims=True) for value in squares], axis=0)
+    average = product[:, patch : patch + 1] * (1.0 / width)
+    spread = spread * (1.0 / width) - jnp.square(average - center)
+    inverse = lax.rsqrt(spread + 1e-06)
+    head = (product[:, 0:patch] - average * column_sum) * inverse + offset_row
+
+    head_high, head_low = split_bf16(head)
+    placed = dot_nn(one_hot, jnp.concatenate([head_high, head_low], axis=1))
+    placed = placed[:, 0:patch] + placed[:, patch:]
+    per = token_rows * token_cols
+    for index in range(token_rows):
+        pieces = [
+            placed[f * per + index * token_cols : f * per + (index + 1) * token_cols, :]
+            for f in range(frames)
+        ]
+        cells_buf[index] = jnp.concatenate(pieces, axis=1)
+
+    slab_peers = (slab > 0).astype(jnp.int32) + (slab < slab_count - 1).astype(jnp.int32)
+    seq_peers = (seq > 0).astype(jnp.int32) + (seq < seq_count - 1).astype(jnp.int32)
+    pl.semaphore_wait(barrier, (1 + slab_peers) * (1 + seq_peers) - 1)
+
+    pair = pltpu.make_async_remote_copy(
+        src_ref=cells_buf.at[1 - half],
+        dst_ref=partner_buf,
+        send_sem=send_sem.at[0],
+        recv_sem=recv_sem.at[0],
+        device_id={"cfg": 1 - half},
+        device_id_type=pl.DeviceIdType.MESH,
+    )
+    pair.start()
+
     for f in range(frames):
         for a in range(2):
             for g in range(lines_buf.shape[2]):
@@ -223,67 +289,6 @@
     now = jnp.full((1, LANES), table_ref[at].astype(F32))
     later = jnp.full((1, LANES), table_ref[at + 1].astype(F32))
     step_size = later / 1000.0 - now / 1000.0
-
-    weight_copy.wait()
-    rhs_buf[0:patch, :] = (w_buf[...].astype(F32) * scale).astype(BF16)
-    rhs_buf[patch : 2 * patch, :] = w_buf[...]
-
-    block = 64
-    blocks = tokens // block
-    product = jnp.zeros((tokens + EXTRA, rhs_buf.shape[0]), F32)
-    centers = [None] * blocks
-    squares = [jnp.zeros((block, LANES), F32)] * blocks
-    for part, hidden_copy in enumerate(loads):
-        low = part * step
-        hidden_copy.wait()
-        product = product + dot_nt(x_buf[:, low : low + step], rhs_buf[:, low : low + step])
-        for index in range(blocks):
-            rows = slice(index * block, (index + 1) * block)
-            if part == 0:
-                total = jnp.zeros((block, LANES), F32)
-                for lane in range(0, step, LANES):
-                    total = total + x_buf[rows, lane : lane + LANES].astype(F32)
-                center = jnp.sum(total, axis=1, keepdims=True) * (1.0 / step)
-                centers[index] = jnp.broadcast_to(center, (block, LANES))
-            square = squares[index]
-            for lane in range(low, low + step, LANES):
-                gap = x_buf[rows, lane : lane + LANES].astype(F32) - centers[index]
-                square = square + gap * gap
-            squares[index] = square
-
-    center = jnp.concatenate([value[:, 0:1] for value in centers], axis=0)
-    spread = jnp.concatenate([jnp.sum(value, axis=1, keepdims=True) for value in squares], axis=0)
-    average = product[0:tokens, 2 * patch : 2 * patch + 1] * (1.0 / width)
-    spread = spread * (1.0 / width) - jnp.square(average - center)
-    inverse = lax.rsqrt(spread + 1e-06)
-    column_sum = product[tokens + 2 : tokens + 3, 0:patch]
-    both = product[tokens : tokens + 1, :] + product[tokens + 1 : tokens + 2, :]
-    offset_row = both[:, patch : 2 * patch]
-    head = (product[0:tokens, 0:patch] - average * column_sum) * inverse + offset_row
-
-    head_high, head_low = split_bf16(head)
-    placed = dot_nn(one_hot, head_high) + dot_nn(one_hot, head_low)
-    per = token_rows * token_cols
-    for index in range(token_rows):
-        pieces = [
-            placed[f * per + index * token_cols : f * per + (index + 1) * token_cols, :]
-            for f in range(frames)
-        ]
-        cells_buf[index] = jnp.concatenate(pieces, axis=1)
-
-    slab_peers = (slab > 0).astype(jnp.int32) + (slab < slab_count - 1).astype(jnp.int32)
-    seq_peers = (seq > 0).astype(jnp.int32) + (seq < seq_count - 1).astype(jnp.int32)
-    pl.semaphore_wait(barrier, (1 + slab_peers) * (1 + seq_peers) - 1)
-
-    pair = pltpu.make_async_remote_copy(
-        src_ref=cells_buf.at[1 - half],
-        dst_ref=partner_buf,
-        send_sem=send_sem.at[0],
-        recv_sem=recv_sem.at[0],
-        device_id={"cfg": 1 - half},
-        device_id_type=pl.DeviceIdType.MESH,
-    )
-    pair.start()
 
     small[-1].wait()
     position = 0
@@ -453,9 +458,9 @@
     )
     block = (token_cols, LANES)
     scratch = [
-        pltpu.VMEM((tokens + EXTRA, width), BF16),
+        pltpu.VMEM((tokens, width), BF16),
         pltpu.VMEM((patch, width), BF16),
-        pltpu.VMEM((2 * patch + EXTRA, width), BF16),
+        pltpu.VMEM((patch + EXTRA, width), BF16),
         pltpu.VMEM(operands[1].shape, jnp.int32),
         pltpu.VMEM(operands[2].shape, F32),
     ]

time: 13.3 us -> 13.7 us (1.030)
  Pallas kernels: 11.1 us -> 11.5 us
    pallas_call x1, Pallas kernels: 11.1 us -> 11.5 us  [per_device(): pl.pallas_call(functools.partial(kernel, sizes), out_shape=pltpu.VMEM((fr...]
where the time goes in v4:
time: 13.7 us; the launch traced here: 13.5 us
  Pallas kernels  11.5 us (84%)
  between operations  1.3 us (9%)
  local copies, waits for them, and re-layouts  0.75 us (5%)
    pallas_call x1, Pallas kernels, per_device(): pl.pallas_call(functools.partial(kernel, sizes), out_shape=pltpu.VMEM((fr...  11.5 us
    unnamed x1, local copies, waits for them, and re-layouts  0.75 us

profile of v4, /device:TPU:1, one launch (start us, length us, event | category | flops | bytes accessed | tf_op | source)
XLA Modules:
  0.0 13.5 jit_solution(3182028820101024750)
XLA Ops:
  1.3 11.5 %guided_step.1 = bf16[2,2,128,384]{3,2,1,0:T(8,128)(2,1)S(1)} custom-call(bf16[1,256,5120]{2,1,0:T(8,128)(2,1)} %hidden_hbm.1, s32[1,256]{1,0:T(1,128)} %bitcast.8, f32[2,2,2048]{2,1,0:T(2,128)} %noisy_hbm.1, bf16[64,5120]{1,0:T(8,128)(2,1)} %bitcast.6, f32[2,5120]{1,0:T(2,128)} %mod_hbm.1, f32[1]{0:T(128)S(6)} %copy.17.guidance_ref, s32[1]{0:T(128)S(6)} %copy.18.index_ref, ...), custom_call_target="tpu_custom_call" | custom-call | tf_op jit(solution)/shard_map/guided_step/pallas_call | solution.py:488
  12.8 0.7 %copy.16 = bf16[2,2,128,384]{3,2,1,0:T(8,128)(2,1)} copy(bf16[2,2,128,384]{3,2,1,0:T(8,128)(2,1)S(1)} %guided_step.1) | data formatting | bytes 786432

commit v5 on v4

--- a/solution.py
+++ b/solution.py
@@ -290,23 +290,6 @@
     later = jnp.full((1, LANES), table_ref[at + 1].astype(F32))
     step_size = later / 1000.0 - now / 1000.0
 
-    small[-1].wait()
-    position = 0
-    for t in range(3):
-        for shifted in range(2):
-            for u in range(4):
-                for e_in in range(2):
-                    dx = (2 - 3 * e_in) if shifted else e_in
-                    for e_out in range(2):
-                        w = dx - e_out + 1
-                        columns = slice(e_out * out_chan, (e_out + 1) * out_chan)
-                        if u < 3 and 0 <= w <= 2:
-                            value = conv_buf[(t * 3 + u) * 3 + w]
-                        else:
-                            value = jnp.zeros((chan, out_chan), BF16)
-                        taps_buf[position : position + chan, columns] = value
-                    position += chan
-
     pair.wait_recv()
     own = cells_buf[half]
     partner = partner_buf[...]
@@ -347,8 +330,22 @@
     for slot in (3, 4, 2, 0, 1):
         pl.when(present(*sends[slot]))(copies[slot].start)
 
-    for slot, (seq_step, slab_step) in enumerate(sends):
-        pl.when(present(-seq_step, -slab_step))(copies[slot].wait_recv)
+    small[-1].wait()
+    position = 0
+    for t in range(3):
+        for shifted in range(2):
+            for u in range(4):
+                for e_in in range(2):
+                    dx = (2 - 3 * e_in) if shifted else e_in
+                    for e_out in range(2):
+                        w = dx - e_out + 1
+                        columns = slice(e_out * out_chan, (e_out + 1) * out_chan)
+                        if u < 3 and 0 <= w <= 2:
+                            value = conv_buf[(t * 3 + u) * 3 + w]
+                        else:
+                            value = jnp.zeros((chan, out_chan), BF16)
+                        taps_buf[position : position + chan, columns] = value
+                    position += chan
 
     lane = lax.broadcasted_iota(jnp.int32, (token_cols, LANES), 1)
     line = lax.broadcasted_iota(jnp.int32, (token_cols, LANES), 0)
@@ -362,40 +359,53 @@
             [turned(block, lane_base - (part * frames + f) * span) for part in range(2)], axis=0
         )
 
-    columns_of = []
-    for center_block, above, below in (
-        (center_buf[1].astype(F32), halo_buf[3].astype(F32), halo_buf[4].astype(F32)),
-        (exact, halo_buf[0].astype(F32), halo_buf[1].astype(F32)),
-    ):
-        for f in range(frames):
-            full = turned(center_block, span - f * span)
-            full = jnp.where(lane >= 2 * span, turned(center_block, -f * span), full)
-            full = jnp.where(lane < span, spread_rows(above, f, 0), full)
-            full = jnp.where(lane >= 3 * span, spread_rows(below, f, 3 * span), full)
-            before = jnp.where(line == 0, 0.0, pltpu.roll(full, 1, 0))
-            after = jnp.where(line == token_cols - 1, 0.0, pltpu.roll(full, token_cols - 1, 0))
-            beside = jnp.where(odd, before, after)
-            lower = (turned(full, -span), turned(beside, -span))
-            columns_of.append(
-                (
-                    (full.astype(BF16), beside.astype(BF16)),
-                    (lower[0].astype(BF16), lower[1].astype(BF16)),
-                )
+    def middle_rows(block, f):
+        return jnp.where(
+            lane >= 2 * span, turned(block, -f * span), turned(block, span - f * span)
+        )
+
+    def tap_rows(full, above, below, f):
+        full = jnp.where(lane < span, spread_rows(above, f, 0), full)
+        full = jnp.where(lane >= 3 * span, spread_rows(below, f, 3 * span), full)
+        before = jnp.where(line == 0, 0.0, pltpu.roll(full, 1, 0))
+        after = jnp.where(line == token_cols - 1, 0.0, pltpu.roll(full, token_cols - 1, 0))
+        beside = jnp.where(odd, before, after)
+        upper = jnp.concatenate([full, beside], axis=1)
+        lower = jnp.concatenate([turned(full, -span), turned(beside, -span)], axis=1)
+        return jnp.concatenate([upper, lower], axis=0).astype(BF16)
+
+    def arrived(slot):
+        seq_step, slab_step = sends[slot]
+        pl.when(present(-seq_step, -slab_step))(copies[slot].wait_recv)
+
+    own_middle = [middle_rows(exact, f) for f in range(frames)]
+    depth = 2 * LANES
+    for slot in (2, 3, 4):
+        arrived(slot)
+    center_block = center_buf[1].astype(F32)
+    above, below = halo_buf[3].astype(F32), halo_buf[4].astype(F32)
+    earlier = [
+        tap_rows(middle_rows(center_block, f), above, below, f) for f in range(frames)
+    ]
+    partial = []
+    for f in range(frames):
+        count = min(2, frames - f)
+        partial.append(
+            dot_nn(
+                jnp.concatenate(earlier[f : f + count], axis=1), taps_buf[0 : count * depth, :]
             )
-    taps = taps_buf[...]
+        )
+    for slot in (0, 1):
+        arrived(slot)
+    above, below = halo_buf[0].astype(F32), halo_buf[1].astype(F32)
+    current = [tap_rows(own_middle[f], above, below, f) for f in range(frames)]
     bias = conv_bias_buf[...]
-    columns = jnp.concatenate(
-        [
-            jnp.concatenate(
-                [piece for t in range(3) for piece in columns_of[f + t][y]], axis=1
-            )
-            for f in range(frames)
-            for y in range(2)
-        ],
-        axis=0,
-    )
-    result = dot_nn(columns, taps)
     for f in range(frames):
+        count = min(2, frames - f)
+        result = partial[f] + dot_nn(
+            jnp.concatenate(current[f + count - frames : f + 1], axis=1),
+            taps_buf[count * depth :, :],
+        )
         for y in range(2):
             first = (f * 2 + y) * token_cols
             for part in range(out_chan // LANES):
@@ -403,7 +413,7 @@
                 for e in range(2):
                     from_lane = e * out_chan + part * LANES
                     wide_buf[part, pl.ds(2 * first + e, token_cols, stride=2), :] = (
-                        result[first : first + token_cols, from_lane : from_lane + LANES]
+                        result[y * token_cols : (y + 1) * token_cols, from_lane : from_lane + LANES]
                         + bias[part : part + 1, :]
                     )
                 out_ref[f, y, :, lanes] = wide_buf[

time: 13.7 us -> 13.6 us (level)
  no operation moved by 1% of the time
where the time goes in v5:
time: 13.6 us; the launch traced here: 13.4 us
  Pallas kernels  11.4 us (84%)
  between operations  1.3 us (10%)
  local copies, waits for them, and re-layouts  0.75 us (6%)
    pallas_call x1, Pallas kernels, per_device(): pl.pallas_call(functools.partial(kernel, sizes), out_shape=pltpu.VMEM((fr...  11.4 us
    unnamed x1, local copies, waits for them, and re-layouts  0.75 us

profile of v5, /device:TPU:1, one launch (start us, length us, event | category | flops | bytes accessed | tf_op | source)
XLA Modules:
  0.0 13.4 jit_solution(6880699230634968504)
XLA Ops:
  1.3 11.4 %guided_step.1 = bf16[2,2,128,384]{3,2,1,0:T(8,128)(2,1)S(1)} custom-call(bf16[1,256,5120]{2,1,0:T(8,128)(2,1)} %hidden_hbm.1, s32[1,256]{1,0:T(1,128)} %bitcast.8, f32[2,2,2048]{2,1,0:T(2,128)} %noisy_hbm.1, bf16[64,5120]{1,0:T(8,128)(2,1)} %bitcast.6, f32[2,5120]{1,0:T(2,128)} %mod_hbm.1, f32[1]{0:T(128)S(6)} %copy.17.guidance_ref, s32[1]{0:T(128)S(6)} %copy.18.index_ref, ...), custom_call_target="tpu_custom_call" | custom-call | tf_op jit(solution)/shard_map/guided_step/pallas_call | solution.py:498
  12.7 0.7 %copy.16 = bf16[2,2,128,384]{3,2,1,0:T(8,128)(2,1)} copy(bf16[2,2,128,384]{3,2,1,0:T(8,128)(2,1)S(1)} %guided_step.1) | data formatting | bytes 786432

commit v6 on v3

--- a/solution.py
+++ b/solution.py
@@ -240,10 +240,8 @@
         for index in range(blocks):
             rows = slice(index * block, (index + 1) * block)
             if part == 0:
-                total = jnp.zeros((block, LANES), F32)
-                for lane in range(0, step, LANES):
-                    total = total + x_buf[rows, lane : lane + LANES].astype(F32)
-                center = jnp.sum(total, axis=1, keepdims=True) * (1.0 / step)
+                total = x_buf[rows, 0:LANES].astype(F32)
+                center = jnp.sum(total, axis=1, keepdims=True) * (1.0 / LANES)
                 centers[index] = jnp.broadcast_to(center, (block, LANES))
             square = squares[index]
             for lane in range(low, low + step, LANES):
@@ -262,7 +260,8 @@
     head = (product[0:tokens, 0:patch] - average * column_sum) * inverse + offset_row
 
     head_high, head_low = split_bf16(head)
-    placed = dot_nn(one_hot, head_high) + dot_nn(one_hot, head_low)
+    placed = dot_nn(one_hot, jnp.concatenate([head_high, head_low], axis=1))
+    placed = placed[:, 0:patch] + placed[:, patch:]
     per = token_rows * token_cols
     for index in range(token_rows):
         pieces = [
@@ -284,23 +283,6 @@
         device_id_type=pl.DeviceIdType.MESH,
     )
     pair.start()
-
-    small[-1].wait()
-    position = 0
-    for t in range(3):
-        for shifted in range(2):
-            for u in range(4):
-                for e_in in range(2):
-                    dx = (2 - 3 * e_in) if shifted else e_in
-                    for e_out in range(2):
-                        w = dx - e_out + 1
-                        columns = slice(e_out * out_chan, (e_out + 1) * out_chan)
-                        if u < 3 and 0 <= w <= 2:
-                            value = conv_buf[(t * 3 + u) * 3 + w]
-                        else:
-                            value = jnp.zeros((chan, out_chan), BF16)
-                        taps_buf[position : position + chan, columns] = value
-                    position += chan
 
     pair.wait_recv()
     own = cells_buf[half]
@@ -342,8 +324,22 @@
     for slot in (3, 4, 2, 0, 1):
         pl.when(present(*sends[slot]))(copies[slot].start)
 
-    for slot, (seq_step, slab_step) in enumerate(sends):
-        pl.when(present(-seq_step, -slab_step))(copies[slot].wait_recv)
+    small[-1].wait()
+    position = 0
+    for t in range(3):
+        for shifted in range(2):
+            for u in range(4):
+                for e_in in range(2):
+                    dx = (2 - 3 * e_in) if shifted else e_in
+                    for e_out in range(2):
+                        w = dx - e_out + 1
+                        columns = slice(e_out * out_chan, (e_out + 1) * out_chan)
+                        if u < 3 and 0 <= w <= 2:
+                            value = conv_buf[(t * 3 + u) * 3 + w]
+                        else:
+                            value = jnp.zeros((chan, out_chan), BF16)
+                        taps_buf[position : position + chan, columns] = value
+                    position += chan
 
     lane = lax.broadcasted_iota(jnp.int32, (token_cols, LANES), 1)
     line = lax.broadcasted_iota(jnp.int32, (token_cols, LANES), 0)
@@ -357,40 +353,53 @@
             [turned(block, lane_base - (part * frames + f) * span) for part in range(2)], axis=0
         )
 
-    columns_of = []
-    for center_block, above, below in (
-        (center_buf[1].astype(F32), halo_buf[3].astype(F32), halo_buf[4].astype(F32)),
-        (exact, halo_buf[0].astype(F32), halo_buf[1].astype(F32)),
-    ):
-        for f in range(frames):
-            full = turned(center_block, span - f * span)
-            full = jnp.where(lane >= 2 * span, turned(center_block, -f * span), full)
-            full = jnp.where(lane < span, spread_rows(above, f, 0), full)
-            full = jnp.where(lane >= 3 * span, spread_rows(below, f, 3 * span), full)
-            before = jnp.where(line == 0, 0.0, pltpu.roll(full, 1, 0))
-            after = jnp.where(line == token_cols - 1, 0.0, pltpu.roll(full, token_cols - 1, 0))
-            beside = jnp.where(odd, before, after)
-            lower = (turned(full, -span), turned(beside, -span))
-            columns_of.append(
-                (
-                    (full.astype(BF16), beside.astype(BF16)),
-                    (lower[0].astype(BF16), lower[1].astype(BF16)),
-                )
+    def middle_rows(block, f):
+        return jnp.where(
+            lane >= 2 * span, turned(block, -f * span), turned(block, span - f * span)
+        )
+
+    def tap_rows(full, above, below, f):
+        full = jnp.where(lane < span, spread_rows(above, f, 0), full)
+        full = jnp.where(lane >= 3 * span, spread_rows(below, f, 3 * span), full)
+        before = jnp.where(line == 0, 0.0, pltpu.roll(full, 1, 0))
+        after = jnp.where(line == token_cols - 1, 0.0, pltpu.roll(full, token_cols - 1, 0))
+        beside = jnp.where(odd, before, after)
+        upper = jnp.concatenate([full, beside], axis=1)
+        lower = jnp.concatenate([turned(full, -span), turned(beside, -span)], axis=1)
+        return jnp.concatenate([upper, lower], axis=0).astype(BF16)
+
+    def arrived(slot):
+        seq_step, slab_step = sends[slot]
+        pl.when(present(-seq_step, -slab_step))(copies[slot].wait_recv)
+
+    own_middle = [middle_rows(exact, f) for f in range(frames)]
+    depth = 2 * LANES
+    for slot in (2, 3, 4):
+        arrived(slot)
+    center_block = center_buf[1].astype(F32)
+    above, below = halo_buf[3].astype(F32), halo_buf[4].astype(F32)
+    earlier = [
+        tap_rows(middle_rows(center_block, f), above, below, f) for f in range(frames)
+    ]
+    partial = []
+    for f in range(frames):
+        count = min(2, frames - f)
+        partial.append(
+            dot_nn(
+                jnp.concatenate(earlier[f : f + count], axis=1), taps_buf[0 : count * depth, :]
             )
-    taps = taps_buf[...]
+        )
+    for slot in (0, 1):
+        arrived(slot)
+    above, below = halo_buf[0].astype(F32), halo_buf[1].astype(F32)
+    current = [tap_rows(own_middle[f], above, below, f) for f in range(frames)]
     bias = conv_bias_buf[...]
-    columns = jnp.concatenate(
-        [
-            jnp.concatenate(
-                [piece for t in range(3) for piece in columns_of[f + t][y]], axis=1
-            )
-            for f in range(frames)
-            for y in range(2)
-        ],
-        axis=0,
-    )
-    result = dot_nn(columns, taps)
     for f in range(frames):
+        count = min(2, frames - f)
+        result = partial[f] + dot_nn(
+            jnp.concatenate(current[f + count - frames : f + 1], axis=1),
+            taps_buf[count * depth :, :],
+        )
         for y in range(2):
             first = (f * 2 + y) * token_cols
             for part in range(out_chan // LANES):
@@ -398,7 +407,7 @@
                 for e in range(2):
                     from_lane = e * out_chan + part * LANES
                     wide_buf[part, pl.ds(2 * first + e, token_cols, stride=2), :] = (
-                        result[first : first + token_cols, from_lane : from_lane + LANES]
+                        result[y * token_cols : (y + 1) * token_cols, from_lane : from_lane + LANES]
                         + bias[part : part + 1, :]
                     )
                 out_ref[f, y, :, lanes] = wide_buf[

time: 13.3 us -> 13.4 us (level)
  no operation moved by 1% of the time
where the time goes in v6:
time: 13.4 us; the launch traced here: 13.2 us
  Pallas kernels  11.2 us (84%)
  between operations  1.3 us (10%)
  local copies, waits for them, and re-layouts  0.75 us (6%)
    pallas_call x1, Pallas kernels, per_device(): pl.pallas_call(functools.partial(kernel, sizes), out_shape=pltpu.VMEM((fr...  11.2 us
    unnamed x1, local copies, waits for them, and re-layouts  0.75 us

profile of v6, /device:TPU:1, one launch (start us, length us, event | category | flops | bytes accessed | tf_op | source)
XLA Modules:
  0.0 13.2 jit_solution(16761127274662881385)
XLA Ops:
  1.3 11.2 %guided_step.1 = bf16[2,2,128,384]{3,2,1,0:T(8,128)(2,1)S(1)} custom-call(bf16[1,256,5120]{2,1,0:T(8,128)(2,1)} %hidden_hbm.1, s32[1,256]{1,0:T(1,128)} %bitcast.8, f32[2,2,2048]{2,1,0:T(2,128)} %noisy_hbm.1, bf16[64,5120]{1,0:T(8,128)(2,1)} %bitcast.6, f32[2,5120]{1,0:T(2,128)} %mod_hbm.1, f32[1]{0:T(128)S(6)} %copy.17.guidance_ref, s32[1]{0:T(128)S(6)} %copy.18.index_ref, ...), custom_call_target="tpu_custom_call" | custom-call | tf_op jit(solution)/shard_map/guided_step/pallas_call | solution.py:492
  12.5 0.7 %copy.16 = bf16[2,2,128,384]{3,2,1,0:T(8,128)(2,1)} copy(bf16[2,2,128,384]{3,2,1,0:T(8,128)(2,1)S(1)} %guided_step.1) | data formatting | bytes 786432

commit v7 on v6

--- a/solution.py
+++ b/solution.py
@@ -108,12 +108,10 @@
                 chunk_sem.at[1 + part],
             )
         )
-    small[0].start()
+    for copy in small[:-1]:
+        copy.start()
     weight_copy.start()
-    loads[0].start()
-    for copy in small[1:-1]:
-        copy.start()
-    for copy in loads[1:]:
+    for copy in loads:
         copy.start()
     small[-1].start()
 

time: 13.4 us -> 13.4 us (level)
  no operation moved by 1% of the time
where the time goes in v7:
time: 13.4 us; the launch traced here: 13.2 us
  Pallas kernels  11.2 us (84%)
  between operations  1.3 us (10%)
  local copies, waits for them, and re-layouts  0.75 us (6%)
    pallas_call x1, Pallas kernels, per_device(): pl.pallas_call(functools.partial(kernel, sizes), out_shape=pltpu.VMEM((fr...  11.2 us
    unnamed x1, local copies, waits for them, and re-layouts  0.75 us

profile of v7, /device:TPU:1, one launch (start us, length us, event | category | flops | bytes accessed | tf_op | source)
XLA Modules:
  0.0 13.2 jit_solution(15119507232035770503)
XLA Ops:
  1.3 11.2 %guided_step.1 = bf16[2,2,128,384]{3,2,1,0:T(8,128)(2,1)S(1)} custom-call(bf16[1,256,5120]{2,1,0:T(8,128)(2,1)} %hidden_hbm.1, s32[1,256]{1,0:T(1,128)} %bitcast.8, f32[2,2,2048]{2,1,0:T(2,128)} %noisy_hbm.1, bf16[64,5120]{1,0:T(8,128)(2,1)} %bitcast.6, f32[2,5120]{1,0:T(2,128)} %mod_hbm.1, f32[1]{0:T(128)S(6)} %copy.17.guidance_ref, s32[1]{0:T(128)S(6)} %copy.18.index_ref, ...), custom_call_target="tpu_custom_call" | custom-call | tf_op jit(solution)/shard_map/guided_step/pallas_call | solution.py:490
  12.5 0.7 %copy.16 = bf16[2,2,128,384]{3,2,1,0:T(8,128)(2,1)} copy(bf16[2,2,128,384]{3,2,1,0:T(8,128)(2,1)S(1)} %guided_step.1) | data formatting | bytes 786432
